TPU v7x, 32 devices: a whole 2x2x4 slice. The times are simulated.
32 devices in a mesh: dp: 2 (over x), seq: 16 (over z, y, core).
Axes of the slice: x: 2, y: 2, z: 4, core: 2. Of those that a mesh axis runs over, the one named last changes fastest.
Arguments:
- tokens: bfloat16 [2, 2048, 1024], P('dp', 'seq'), may hold values from -6 to 6
- in_gain: float32 [1024], replicated, may hold values from 0.1 to 1.9
- w_proj: bfloat16 [1024, 4096], replicated, may hold values from -0.1875 to 0.1875
- out_gain: float32 [1024], replicated, may hold values from 0.1 to 1.9
- w_out: bfloat16 [1024, 1024], replicated, may hold values from -0.1875 to 0.1875
- rab_slope: float32 [8], replicated, may hold values from -1 to 0.2
- hist_blocks: int32 [2, 3], P('dp'), may hold values from 1 to 10, 16 in all within a row
- hist_tail: int32 [2, 3], P('dp'), may hold values from 1 to 128
- node_table: bfloat16 [512, 1024], P('dp'), may hold values from -0.1875 to 0.1875
- subtree_map: int32 [8], replicated, may hold values from 0 to 7, each once
- beam_nodes: int32 [6, 1024], P('dp', 'seq'), may hold values from 0 to 511
Outputs:
- layer_out: bfloat16 [2, 2048, 1024], P('dp', 'seq')
- beam_scores: float32 [6, 1024], P('dp', 'seq')
Inputs may be any that keep to these rules, and one draw needn't show every extreme that they name: `hist_blocks`: each row sums to 16; its largest entry is exactly 10. `subtree_map`: a permutation of 0 to 7.
All inputs are finite; a program needn't handle non-finite values.
Results may differ from a plain program's by a relative error of at most 0.0059.
Values may be sent and summed in bfloat16 or wider, within the bound.
A program may use at most 128 MiB of HBM per device.

v0:
```python
import math

import jax
import jax.numpy as jnp
from jax import lax
from jax.sharding import PartitionSpec as P

BLK = 128
SUBT = 64
USERS = 3


def layer_norm(rows):
    centred = rows - jnp.mean(rows, axis=-1, keepdims=True)
    spread = jnp.mean(centred * centred, axis=-1, keepdims=True)
    return centred * lax.rsqrt(spread + 1e-05)


def user_table(blocks, tail_len):
    starts = jnp.cumsum(blocks) - blocks
    lengths = (blocks - 1) * BLK + tail_len
    return (starts, lengths)


def segments(blocks, tail_len, positions):
    starts, lengths = user_table(blocks, tail_len)
    block_of = jnp.floor_divide(positions, BLK)
    owning = jnp.sum((block_of[:, None] >= starts[None, :]).astype(jnp.int32), axis=1) - 1
    onehot = (owning[:, None] == jnp.arange(USERS, dtype=jnp.int32)[None, :]).astype(jnp.int32)
    first_pos = jnp.sum(onehot * starts[None, :], axis=1) * BLK
    user_len = jnp.sum(onehot * lengths[None, :], axis=1)
    is_live = (owning >= 0) & (positions - first_pos < user_len)
    return jnp.where(is_live, owning, -1)


def attend(queries, query_pos, query_seg, key_rows, value_rows, key_pos, key_seg, rab_slope):
    scores = jnp.einsum("qhd,khd->hqk", queries, key_rows, preferred_element_type=jnp.float32)
    scores = scores * queries.shape[-1] ** (-0.5)
    gap = query_pos[:, None] - key_pos[None, :]
    allowed = (query_seg[:, None] == key_seg[None, :]) & (query_seg[:, None] >= 0) & (gap >= 0)
    bias = rab_slope[:, None, None] * jnp.log1p(jnp.maximum(gap, 0).astype(jnp.float32))[None]
    weights = jnp.where(allowed[None], jax.nn.silu(scores + bias), 0.0).astype(jnp.bfloat16)
    return jnp.einsum("hqk,khd->qhd", weights, value_rows, preferred_element_type=jnp.float32)


def head_attend(query_recv, kv_recv, blocks, tail_len, slope_one, replicas, residue, tok_dev, back):
    n_src, per_src, head_dim = query_recv.shape
    total_q = n_src * per_src
    tok_dp = n_src * tok_dev
    query_flat = query_recv.reshape(total_q, 1, head_dim)
    query_pos_all = jnp.arange(total_q, dtype=jnp.int32) * replicas + residue
    query_seg_all = segments(blocks, tail_len, query_pos_all)
    kv_flat = kv_recv.reshape(tok_dp, 2 * head_dim)
    kv_pad = jnp.concatenate([jnp.zeros((back, 2 * head_dim), kv_flat.dtype), kv_flat], axis=0)
    key_pos_pad = jnp.arange(-back, tok_dp, dtype=jnp.int32)
    key_seg_all = segments(blocks, tail_len, jnp.arange(tok_dp, dtype=jnp.int32))
    key_seg_pad = jnp.concatenate([jnp.full((back,), -1, jnp.int32), key_seg_all], axis=0)
    qblock = math.gcd(512, total_q)
    span = back + qblock * replicas

    def per_block(index):
        first = index * qblock
        key_start = first * replicas
        queries = lax.dynamic_slice_in_dim(query_flat, first, qblock, 0)
        query_pos = lax.dynamic_slice_in_dim(query_pos_all, first, qblock, 0)
        query_seg = lax.dynamic_slice_in_dim(query_seg_all, first, qblock, 0)
        kv_here = lax.dynamic_slice_in_dim(kv_pad, key_start, span, 0)
        key_rows = kv_here[:, :head_dim].reshape(span, 1, head_dim)
        value_rows = kv_here[:, head_dim:].reshape(span, 1, head_dim)
        key_pos = lax.dynamic_slice_in_dim(key_pos_pad, key_start, span, 0)
        key_seg = lax.dynamic_slice_in_dim(key_seg_pad, key_start, span, 0)
        return attend(
            queries, query_pos, query_seg, key_rows, value_rows, key_pos, key_seg, slope_one
        )

    result = lax.map(per_block, jnp.arange(total_q // qblock, dtype=jnp.int32))
    return result.reshape(n_src, per_src, head_dim)


def body(
    tokens,
    in_gain,
    w_proj,
    out_gain,
    w_out,
    rab_slope,
    hist_blocks,
    hist_tail,
    node_table,
    subtree_map,
    beam_nodes,
):
    x_rows = tokens[0]
    tok_dev, width = x_rows.shape
    heads = rab_slope.shape[0]
    head_dim = width // heads
    n_seq = lax.axis_size("seq")
    seq_index = lax.axis_index("seq")
    blocks = hist_blocks[0]
    tail_len = hist_tail[0]
    normed = (layer_norm(x_rows.astype(jnp.float32)) * in_gain).astype(jnp.bfloat16)
    proj = jax.nn.silu(jnp.dot(normed, w_proj, preferred_element_type=jnp.float32)).astype(
        jnp.bfloat16
    )
    gate_rows = proj[:, :width]
    queries = proj[:, width : 2 * width].reshape(tok_dev, heads, head_dim)
    key_value = proj[:, 2 * width :]
    most_blocks = n_seq // 2 * tok_dev // BLK + 2
    replicas = n_seq // heads
    per_src = tok_dev // replicas
    my_head = seq_index // replicas
    residue = seq_index % replicas
    query_send = queries.reshape(per_src, replicas, heads, head_dim).transpose(2, 1, 0, 3)
    query_send = query_send.reshape(heads * replicas, per_src, head_dim)
    kv_heads = key_value.reshape(tok_dev, 2, heads, head_dim).transpose(2, 0, 1, 3)
    kv_heads = kv_heads.reshape(heads, tok_dev, 2 * head_dim)
    kv_send = jnp.repeat(kv_heads, replicas, axis=0)
    query_recv, kv_recv = (
        lax.all_to_all(query_send, "seq", split_axis=0, concat_axis=0, tiled=True),
        lax.all_to_all(kv_send, "seq", split_axis=0, concat_axis=0, tiled=True),
    )
    slope_one = lax.dynamic_slice_in_dim(rab_slope, my_head, 1, 0)
    result = head_attend(
        query_recv,
        kv_recv,
        blocks,
        tail_len,
        slope_one,
        replicas,
        residue,
        tok_dev,
        most_blocks * BLK,
    )
    returned = lax.all_to_all(result, "seq", split_axis=0, concat_axis=0, tiled=True)
    mixed = (
        returned.reshape(heads, replicas, per_src, head_dim)
        .transpose(2, 1, 0, 3)
        .reshape(tok_dev, width)
    )
    gated = (layer_norm(mixed) * out_gain * gate_rows.astype(jnp.float32)).astype(jnp.bfloat16)
    layer_rows = (
        x_rows.astype(jnp.float32) + jnp.dot(gated, w_out, preferred_element_type=jnp.float32)
    ).astype(jnp.bfloat16)
    starts, lengths = user_table(blocks, tail_len)
    local_last = starts * BLK + lengths - 1 - seq_index * tok_dev
    picker = (jnp.arange(tok_dev, dtype=jnp.int32)[None, :] == local_last[:, None]).astype(
        jnp.bfloat16
    )
    state_part = jnp.dot(picker, layer_rows, preferred_element_type=jnp.float32)
    dp_index = lax.axis_index("dp")
    state_rows = lax.psum(state_part, "seq").astype(jnp.bfloat16)
    all_states, all_ids = (
        lax.all_gather(state_rows, "dp", axis=0, tiled=True),
        lax.all_gather(beam_nodes, "dp", axis=0, tiled=True),
    )
    nodes_here = node_table.shape[0]
    stored = jnp.take(subtree_map, all_ids // SUBT) * SUBT + all_ids % SUBT
    local_rows = stored - dp_index * nodes_here
    owned = (local_rows >= 0) & (local_rows < nodes_here)
    local_scores = lax.dot_general(
        all_states, node_table, (((1,), (1,)), ((), ())), preferred_element_type=jnp.float32
    )
    picked = jnp.take_along_axis(local_scores, jnp.clip(local_rows, 0, nodes_here - 1), axis=1)
    picked = jnp.where(owned, picked, 0.0)
    beam_scores = lax.psum_scatter(picked, "dp", scatter_dimension=0, tiled=True)
    return (layer_rows[None], beam_scores)


def solution(mesh):
    placed = (
        P("dp", "seq", None),
        P(),
        P(),
        P(),
        P(),
        P(),
        P("dp", None),
        P("dp", None),
        P("dp", None),
        P(),
        P("dp", "seq"),
    )
    return jax.shard_map(
        body,
        mesh=mesh,
        in_specs=placed,
        out_specs=(P("dp", "seq", None), P("dp", "seq")),
        check_vma=False,
    )
```

profile of v0, /device:TPU:0, one launch (start us, length us, event | category | flops | bytes accessed | tf_op | source)
XLA Modules:
  0.0 173.2 jit_solution(17398313686638196095)
XLA Ops:
  0.6 1.2 convert_reduce_fusion
  1.9 1.2 fusion.23
  3.0 4.9 %multiply_convert_fusion = bf16[128,4096]{1,0:T(8,128)(2,1)S(1)} fusion(bf16[1024,4096]{1,0:T(8,128)(2,1)} %param.15, bf16[1,128,1024]{2,1,0:T(8,128)(2,1)} %param.13, f32[1024]{0:T(1024)} %param.14, f32[128]{0:T(128)S(1)} %add_rsqrt_fusion.1, f32[128]{0:T(128)S(1)} %broadcast_multiply_fusion.1), kind=kOutput, calls=%fused_computation.23 | convolution fusion | flops 1077018624 | bytes 9704448 | tf_op jit(solution)/shard_map/dot_general | solution.py:102
  8.1 0.1 copy.39
  8.2 0.8 copy-done.3
  9.0 0.5 copy.26
  9.4 0.2 copy.27
  9.7 1.1 broadcast_in_dim.33
  10.7 7.4 %all-to-all-start = ((bf16[16,128,256]{2,1,0:T(8,128)(2,1)}), bf16[16,128,256]{2,1,0:T(8,128)(2,1)S(1)}, u32[]{:S(2)}, u32[]{:S(2)}) async-start(bf16[16,128,256]{2,1,0:T(8,128)(2,1)} %bitcast.129), calls=%async_computation | async-start | bytes 2097152 | tf_op jit(solution)/shard_map/all_to_all | solution.py:120
  18.2 0.2 reduce-window.4
  18.3 1.0 slice_bitcast_fusion.1
  19.4 0.8 copy.28
  20.3 0.1 convert_reduce_fusion.1
  20.4 0.1 select_reduce_fusion.1
  20.5 20.6 %all-to-all-done = bf16[16,128,256]{2,1,0:T(8,128)(2,1)S(1)} async-done(((bf16[16,128,256]{2,1,0:T(8,128)(2,1)}), bf16[16,128,256]{2,1,0:T(8,128)(2,1)S(1)}, u32[]{:S(2)}, u32[]{:S(2)}) %all-to-all-start) | async-done | bytes 1048608 | tf_op jit(solution)/shard_map/all_to_all | solution.py:120
  41.1 6.9 %all-to-all-start.1 = ((bf16[16,64,128]{2,1,0:T(8,128)(2,1)}), bf16[16,64,128]{2,1,0:T(8,128)(2,1)}, u32[]{:S(2)}, u32[]{:S(2)}) async-start(bf16[16,64,128]{2,1,0:T(8,128)(2,1)} %bitcast.17), calls=%async_computation.1 | async-start | bytes 524288 | tf_op jit(solution)/shard_map/all_to_all | solution.py:119
  48.1 0.6 dynamic_slice.46
  48.8 1.3 concatenate.6
  50.1 8.0 %all-to-all-done.1 = bf16[16,64,128]{2,1,0:T(8,128)(2,1)} async-done(((bf16[16,64,128]{2,1,0:T(8,128)(2,1)}), bf16[16,64,128]{2,1,0:T(8,128)(2,1)}, u32[]{:S(2)}, u32[]{:S(2)}) %all-to-all-start.1) | async-done | bytes 262176 | tf_op jit(solution)/shard_map/all_to_all | solution.py:119
  58.1 20.0 %while.12 = (s32[]{:T(128)}, f32[2,512,1,128]{3,1,0,2:T(8,128)}, s32[2]{0:T(128)S(1)}, bf16[3328,256]{1,0:T(8,128)(2,1)}, s32[1024]{0:T(1024)S(1)}, /*index=5*/s...) while((s32[]{:T(128)}, f32[2,512,1,128]{3,1,0,2:T(8,128)}, ...), condition=%wide.region_10.11_spmd, body=%wide.region_9.10_spmd.sunk | while | flops 622854656 | bytes 6887261 | solution.py:76
  58.1 0.6 dynamic_slice.61
  60.3 6.8 %fusion.78 = f32[1,512,1,128]{1,3,2,0:T(8,128)S(1)} fusion(f32[]{:T(128)} %bitcast.122, s32[2304]{0:T(1024)S(1)} %dynamic_slice.62, s32[512]{0:T(512)S(1)} %dynamic_slice.63, s32[2304]{0:T(1024)S(1)} %dynamic_slice.64, s32[512]{0:T(512)S(1)} %get-tuple-element.223, pred[512]{0:T(512)(128)(4,1)S(1)} %get-tuple-element.224, ...), kind=kOutput, calls=%fused_computation.12.clone.1 | convolution fusion | flops 622854144 | bytes 1598464 | tf_op jit(solution)/shard_map/while/body/eval_jaxpr/hqk,khd->qhd/dot_general | solution.py:43
  67.1 0.1 copy.45
  67.3 0.8 copy-done.5
  68.1 0.6 dynamic_slice.61
  70.3 6.8 %fusion.78 = f32[1,512,1,128]{1,3,2,0:T(8,128)S(1)} fusion(f32[]{:T(128)} %bitcast.122, s32[2304]{0:T(1024)S(1)} %dynamic_slice.62, s32[512]{0:T(512)S(1)} %dynamic_slice.63, s32[2304]{0:T(1024)S(1)} %dynamic_slice.64, s32[512]{0:T(512)S(1)} %get-tuple-element.223, pred[512]{0:T(512)(128)(4,1)S(1)} %get-tuple-element.224, ...), kind=kOutput, calls=%fused_computation.12.clone.1 | convolution fusion | flops 622854144 | bytes 1598464 | tf_op jit(solution)/shard_map/while/body/eval_jaxpr/hqk,khd->qhd/dot_general | solution.py:43
  77.1 0.1 copy.45
  77.3 0.8 copy-done.5
  78.1 3.7 %all-to-all-start.2 = ((f32[16,64,128]{2,1,0:T(8,128)}), f32[16,64,128]{2,1,0:T(8,128)S(1)}, u32[]{:S(2)}, u32[]{:S(2)}) async-start(f32[16,64,128]{2,1,0:T(8,128)} %bitcast.134), calls=%async_computation.2 | async-start | bytes 1048576 | tf_op jit(solution)/shard_map/all_to_all | solution.py:134
  81.8 4.3 %all-gather = s32[2,3,64]{2,1,0:T(4,128)S(1)} all-gather(s32[1,3,64]{2,1,0:T(4,128)S(1)} %bitcast.137), channel_id=1, replica_groups=mesh['dp'=2,'seq'=16] {'dp'}, dimensions={0}, use_global_device_ids=true | all-gather | bytes 2304 | tf_op jit(solution)/shard_map/all_gather | solution.py:154
  86.3 2.7 %gather_fusion = s32[384]{0:T(512)S(1)} fusion(s32[8]{0:T(128)S(1)} %copy-done.1, s32[1024]{0:T(1024)S(1)} %pad_clamp_fusion), kind=kCustom, calls=%fused_computation | custom fusion | bytes 4608 | tf_op jit(solution)/shard_map/jit(_take)/gather | solution.py:157
  89.2 0.6 dynamic-slice
  90.4 5.8 %all-to-all-done.2 = f32[16,64,128]{2,1,0:T(8,128)S(1)} async-done(((f32[16,64,128]{2,1,0:T(8,128)}), f32[16,64,128]{2,1,0:T(8,128)S(1)}, u32[]{:S(2)}, u32[]{:S(2)}) %all-to-all-start.2) | async-done | bytes 524320 | tf_op jit(solution)/shard_map/all_to_all | solution.py:134
  96.2 0.3 copy.30
  96.5 0.1 reduce_sum.98
  96.7 0.2 multiply_reduce_fusion
  96.9 0.1 copy.31
  97.0 0.1 copy.32
  97.1 0.1 rsqrt.21
  97.2 0.1 div.79
  97.4 1.6 fusion.19
  99.0 0.2 fusion.56
  99.2 60.1 %psum.7 = bf16[3,1024]{1,0:T(4,128)(2,1)S(1)} all-reduce(f32[3,1024]{1,0:T(4,128)S(1)} %fusion.56), channel_id=1, replica_groups=mesh['dp'=2,'seq'=16] {'seq'}, use_global_device_ids=true, to_apply=%region_13.14 | all-reduce | flops 3072 | bytes 18432 | tf_op jit(solution)/shard_map/psum | solution.py:151
  159.2 4.4 %all-gather.1 = bf16[2,3,1024]{2,1,0:T(4,128)(2,1)S(1)} all-gather(bf16[1,3,1024]{2,1,0:T(4,128)(2,1)S(1)} %bitcast.136), channel_id=1, replica_groups=mesh['dp'=2,'seq'=16] {'dp'}, dimensions={0}, use_global_device_ids=true | all-gather | bytes 18432 | tf_op jit(solution)/shard_map/all_gather | solution.py:153
  163.6 1.3 fusion.65
  164.9 2.8 %gather_fusion.1 = f32[384]{0:T(512)S(1)} fusion(f32[6,256]{1,0:T(8,128)S(1)} %fusion.65, s32[384]{0:T(512)S(1)} %reshape.231), kind=kCustom, calls=%fused_computation.1 | custom fusion | bytes 6144 | tf_op jit(solution)/shard_map/jit(take_along_axis)/gather | solution.py:163
  167.7 4.9 %all-reduce.2 = f32[6,64]{1,0:T(8,128)S(1)} all-reduce(f32[6,64]{1,0:T(8,128)S(1)} %select_select_fusion), channel_id=2, replica_groups=mesh['dp'=2,'seq'=16] {'dp'}, use_global_device_ids=true, to_apply=%region_14.15.clone | all-reduce | flops 384 | bytes 3072
  172.6 0.6 constant_dynamic-slice_fusion
  (67 shorter events, 1.5 us)
Async XLA Ops:
  0.6 96.7 %copy-start = (bf16[1024,1024]{1,0:T(8,128)(2,1)S(1)}, bf16[1024,1024]{1,0:T(8,128)(2,1)}, u32[]{:S(2)}) copy-start(bf16[1024,1024]{1,0:T(8,128)(2,1)} %param.17) | copy-start | bytes 6291460
  8.0 1.0 copy-start.3
  8.0 10.2 %copy-start.10 = (s32[1,3]{1,0:T(1,128)S(1)}, s32[1,3]{1,0:T(1,128)}, u32[]{:S(2)}) copy-start(s32[1,3]{1,0:T(1,128)} %param.19) | copy-start | bytes 40
  8.0 12.2 %copy-start.9 = (s32[1,3]{1,0:T(1,128)S(1)}, s32[1,3]{1,0:T(1,128)}, u32[]{:S(2)}) copy-start(s32[1,3]{1,0:T(1,128)} %param.20) | copy-start | bytes 40
  8.1 40.0 %copy-start.11 = (f32[8]{0:T(128)S(1)}, f32[8]{0:T(128)}, u32[]{:S(2)}) copy-start(f32[8]{0:T(128)} %param.18) | copy-start | bytes 100
  10.7 30.3 %all-to-all-start = ((bf16[16,128,256]{2,1,0:T(8,128)(2,1)}), bf16[16,128,256]{2,1,0:T(8,128)(2,1)S(1)}, u32[]{:S(2)}, u32[]{:S(2)}) async-start(bf16[16,128,256]{2,1,0:T(8,128)(2,1)} %bitcast.129), calls=%async_computation | async-start | bytes 2097152 | tf_op jit(solution)/shard_map/all_to_all | solution.py:120
  41.1 17.0 %all-to-all-start.1 = ((bf16[16,64,128]{2,1,0:T(8,128)(2,1)}), bf16[16,64,128]{2,1,0:T(8,128)(2,1)}, u32[]{:S(2)}, u32[]{:S(2)}) async-start(bf16[16,64,128]{2,1,0:T(8,128)(2,1)} %bitcast.17), calls=%async_computation.1 | async-start | bytes 524288 | tf_op jit(solution)/shard_map/all_to_all | solution.py:119
  58.1 23.7 %copy-start.8 = (s32[3,64]{1,0:T(4,128)S(1)}, s32[3,64]{1,0:T(4,128)}, u32[]{:S(2)}) copy-start(s32[3,64]{1,0:T(4,128)} %param.23) | copy-start | bytes 2308
  58.1 28.2 %copy-start.1 = (s32[8]{0:T(128)S(1)}, s32[8]{0:T(128)}, u32[]{:S(2)}) copy-start(s32[8]{0:T(128)} %param.22) | copy-start | bytes 100
  60.3 6.9 %copy-start.4 = (f32[2,512,1,128]{3,1,0,2:T(8,128)S(1)}, f32[2,512,1,128]{3,1,0,2:T(8,128)}, u32[]{:S(2)}) copy-start(f32[2,512,1,128]{3,1,0,2:T(8,128)} %get-tuple-element.243) | copy-start | bytes 1572868 | tf_op jit(solution)/shard_map/while
  67.3 0.8 copy-start.5
  70.3 6.9 %copy-start.4 = (f32[2,512,1,128]{3,1,0,2:T(8,128)S(1)}, f32[2,512,1,128]{3,1,0,2:T(8,128)}, u32[]{:S(2)}) copy-start(f32[2,512,1,128]{3,1,0,2:T(8,128)} %get-tuple-element.243) | copy-start | bytes 1572868 | tf_op jit(solution)/shard_map/while
  77.3 0.8 copy-start.5
  78.1 11.1 %copy-start.12 = (u32[32]{0:T(128)S(1)}, u32[32]{0:T(128)}, u32[]{:S(2)}) copy-start(u32[32]{0:T(128)} %constant.242) | copy-start | bytes 388
  78.1 19.3 %copy-start.2 = (bf16[1,128,1024]{2,1,0:T(8,128)(2,1)S(1)}, bf16[1,128,1024]{2,1,0:T(8,128)(2,1)}, u32[]{:S(2)}) copy-start(bf16[1,128,1024]{2,1,0:T(8,128)(2,1)} %param.13) | copy-start | bytes 786436
  78.1 19.3 %copy-start.7 = (f32[1024]{0:T(1024)S(1)}, f32[1024]{0:T(1024)}, u32[]{:S(2)}) copy-start(f32[1024]{0:T(1024)} %param.16) | copy-start | bytes 12292
  78.1 18.1 %all-to-all-start.2 = ((f32[16,64,128]{2,1,0:T(8,128)}), f32[16,64,128]{2,1,0:T(8,128)S(1)}, u32[]{:S(2)}, u32[]{:S(2)}) async-start(f32[16,64,128]{2,1,0:T(8,128)} %bitcast.134), calls=%async_computation.2 | async-start | bytes 1048576 | tf_op jit(solution)/shard_map/all_to_all | solution.py:134
  98.9 74.3 %copy-start.6 = (bf16[128,1024]{1,0:T(8,128)(2,1)}, bf16[128,1024]{1,0:T(8,128)(2,1)S(1)}, u32[]{:S(2)}) copy-start(bf16[128,1024]{1,0:T(8,128)(2,1)S(1)} %fusion.19) | copy-start | bytes 786436
where the time goes:
time: 174 us; the launch traced here: 173 us
  blocking collectives  73.7 us (42%)
  waiting for transfers between devices  34.4 us (20%)
  matrix products  21.5 us (12%)
  starting transfers between devices  18 us (10%)
  local copies, waits for them, and re-layouts  17.7 us (10%)
  other arithmetic  3.57 us (2%)
  loops' own time  2.72 us (2%)
    psum x1, blocking collectives, body(): state_rows = lax.psum(state_part, 'seq').astype(jnp.bfloat16)  60.1 us
    all_to_all x1, waiting for transfers between devices, body(): lax.all_to_all(kv_send, 'seq', split_axis=0, concat_axis=0, tiled=True)  20.6 us
    dot_general x2, matrix products, attend(): jnp.einsum('hqk,khd->qhd', weights, value_rows, preferred_element_type=jn...  13.6 us
    all_to_all x1, waiting for transfers between devices, body(): lax.all_to_all(query_send, 'seq', split_axis=0, concat_axis=0, tiled=True)  8.03 us
    all_to_all x1, starting transfers between devices, body(): lax.all_to_all(kv_send, 'seq', split_axis=0, concat_axis=0, tiled=True)  7.39 us
    all_to_all x1, starting transfers between devices, body(): lax.all_to_all(query_send, 'seq', split_axis=0, concat_axis=0, tiled=True)  6.92 us
    all_to_all x1, waiting for transfers between devices, body(): lax.all_to_all(result, 'seq', split_axis=0, concat_axis=0, tiled=True)  5.82 us
    dot_general x1, matrix products, body(): jnp.dot(normed, w_proj, preferred_element_type=jnp.float32)  4.93 us
  transfers between devices with their start and end apart: 3, of which 3 were waited for; matrix products, arithmetic and copies ran while one was open for 5% of the time, Pallas kernels for 0%

commit v1 on v0

v1 whole, which is shorter than its diff:
```python
import functools

import jax
import jax.numpy as jnp
from jax import lax
from jax.experimental import pallas as pl
from jax.experimental.pallas import tpu as pltpu
from jax.sharding import PartitionSpec as P

BLK = 128
SUBT = 64
USERS = 3
LANES = 128
MESH = pl.DeviceIdType.MESH
OFF = -1e30


def layer_norm(rows):
    centred = rows - jnp.mean(rows, axis=-1, keepdims=True)
    spread = jnp.mean(centred * centred, axis=-1, keepdims=True)
    return centred * lax.rsqrt(spread + 1e-05)


def silu_of_half(half):
    return half + half * jnp.tanh(half)


def far_first(count):
    order = []
    for step in range(count // 2):
        for offset in (count // 2 - step, count // 2 + step):
            if 0 < offset < count and offset not in order:
                order.append(offset)
    return order


def layer_kernel(
    n_dp,
    n_seq,
    x_ref,
    in_gain_ref,
    w_proj_ref,
    out_gain_ref,
    w_out_ref,
    slope_ref,
    blocks_ref,
    tail_ref,
    table_ref,
    map_ref,
    beam_ref,
    layer_ref,
    scores_ref,
    w_buf,
    w_out_buf,
    table_buf,
    sent,
    gate,
    kv,
    query,
    result,
    mix,
    bias,
    part_sent,
    part_recv,
    onehot,
    w_sem,
    w_out_sem,
    table_sem,
    table_send,
    table_recv,
    kv_send,
    kv_recv,
    fwd_send,
    q_send,
    q_recv,
    r_send,
    r_recv,
    p_send,
    p_recv,
):
    tok, width = x_ref.shape[1:]
    heads, _, head_dim = mix.shape
    half = query.shape[1]
    window = bias.shape[1] // tok
    nodes = table_ref.shape[0]
    chunks = n_dp * nodes // LANES
    me = lax.axis_index("seq")
    dp = lax.axis_index("dp")
    chip, core = me // 2, me % 2
    sibling = chip * 2 + (1 - core)

    def remote(src, dst, send_sem, recv_sem, where):
        return pltpu.make_async_remote_copy(
            src_ref=src,
            dst_ref=dst,
            send_sem=send_sem,
            recv_sem=recv_sem,
            device_id=where,
            device_id_type=MESH,
        )

    order = (2, 3, 1, 0)
    w_copies = {
        part: pltpu.make_async_copy(
            w_proj_ref.at[:, pl.ds(part * width, width)], w_buf.at[part], w_sem.at[part]
        )
        for part in order
    }
    for part in order:
        w_copies[part].start()

    barrier = pltpu.get_barrier_semaphore()
    for step in range(1, n_seq):
        pl.semaphore_signal(
            barrier, inc=1, device_id={"seq": (me + step) % n_seq}, device_id_type=MESH
        )
    for step in range(1, n_dp):
        pl.semaphore_signal(
            barrier, inc=1, device_id={"dp": (dp + step) % n_dp}, device_id_type=MESH
        )

    x_rows = x_ref[0].astype(jnp.float32)
    normed = (layer_norm(x_rows) * in_gain_ref[...]).astype(jnp.bfloat16)

    def project(part, store):
        w_copies[part].wait()
        for piece in range(heads // 2):
            columns = pl.ds(piece * 2 * head_dim, 2 * head_dim)
            out = jnp.dot(normed, w_buf[part, :, columns], preferred_element_type=jnp.float32)
            store(piece, silu_of_half(0.5 * out).astype(jnp.bfloat16))

    def store_heads(slot):
        def store(piece, rows):
            sent[slot, 2 * piece] = rows[:, :head_dim]
            sent[slot, 2 * piece + 1] = rows[:, head_dim:]

        return store

    chip_order = far_first(heads)
    waits = []
    for which in range(2):
        slot = which + 1
        project(slot + 1, store_heads(slot))
        if which == 0:
            pl.semaphore_wait(barrier, n_seq - 1 + n_dp - 1)
        for step in chip_order:
            head = (chip + step) % heads
            copy = remote(
                sent.at[slot, head],
                kv.at[which, me],
                kv_send.at[which, step],
                kv_recv.at[which, me],
                {"seq": head * 2 + core},
            )
            copy.start()
            waits.append(copy)
        copy = remote(
            sent.at[slot, chip],
            kv.at[which, me],
            kv_send.at[which, 0],
            kv_recv.at[which, me],
            {"seq": sibling},
        )
        copy.start()
        waits.append(copy)
        pltpu.make_async_copy(
            sent.at[slot, chip], kv.at[which, me], kv_recv.at[which, me]
        ).start()

    project(1, store_heads(0))
    for step in chip_order:
        head = (chip + step) % heads
        for part in range(2):
            copy = remote(
                sent.at[0, head, pl.ds(part * half, half)],
                query.at[me],
                q_send.at[2 * step + part],
                q_recv.at[me],
                {"seq": head * 2 + part},
            )
            copy.start()
            waits.append(copy)
    copy = remote(
        sent.at[0, chip, pl.ds((1 - core) * half, half)],
        query.at[me],
        q_send.at[0],
        q_recv.at[me],
        {"seq": sibling},
    )
    copy.start()
    waits.append(copy)
    pltpu.make_async_copy(
        sent.at[0, chip, pl.ds(core * half, half)], query.at[me], q_recv.at[me]
    ).start()

    for step in range(1, n_dp):
        copy = remote(
            table_ref,
            table_buf.at[dp],
            table_send.at[step],
            table_recv.at[dp],
            {"dp": (dp + step) % n_dp},
        )
        copy.start()
        waits.append(copy)
    pltpu.make_async_copy(table_ref, table_buf.at[dp], table_sem).start()
    w_out_copy = pltpu.make_async_copy(w_out_ref, w_out_buf, w_out_sem)
    w_out_copy.start()

    def store_gate(piece, rows):
        gate[:, pl.ds(piece * 2 * head_dim, 2 * head_dim)] = rows

    project(0, store_gate)

    row = lax.broadcasted_iota(jnp.int32, bias.shape, 0)
    column = lax.broadcasted_iota(jnp.int32, bias.shape, 1)
    gap = (window - 1) * tok + core * half + row - column
    slope = slope_ref[chip]
    logs = jnp.log(1.0 + jnp.maximum(gap, 0).astype(jnp.float32))
    bias[...] = jnp.where(gap >= 0, (0.5 * slope) * logs, OFF)

    beams = beam_ref[...]
    subtree = beams >> 6
    base = jnp.zeros_like(beams)
    for index in range(map_ref.shape[0]):
        base = jnp.where(subtree == index, map_ref[index], base)
    stored = base * SUBT + (beams & (SUBT - 1))
    per_user = beams.shape[1]
    stored_row = jnp.concatenate([stored[u : u + 1] for u in range(USERS)], axis=1)
    node = lax.broadcasted_iota(jnp.int32, onehot.shape, 0)
    onehot[...] = jnp.where(node == stored_row, 1.0, 0.0).astype(jnp.bfloat16)

    starts = [0, blocks_ref[0, 0], blocks_ref[0, 0] + blocks_ref[0, 1]]
    lengths = [(blocks_ref[0, u] - 1) * BLK + tail_ref[0, u] for u in range(USERS)]

    def attend(block):
        pltpu.make_async_copy(query.at[block], query.at[block], q_recv.at[block]).wait()
        count = min(block + 1, window)
        low = block + 1 - count
        keys = kv[0, low : block + 1].reshape(count * tok, head_dim)
        values = kv[1, low : block + 1].reshape(count * tok, head_dim)
        first = jnp.where(block >= starts[1], starts[1], 0)
        length = jnp.where(block >= starts[1], lengths[1], lengths[0])
        first = jnp.where(block >= starts[2], starts[2], first)
        length = jnp.where(block >= starts[2], lengths[2], length)
        column = lax.broadcasted_iota(jnp.int32, (1, count * tok), 1) + low * tok
        seen = jnp.where(column >= first * tok, 0.0, OFF)
        scores = lax.dot_general(
            query[block], keys, (((1,), (1,)), ((), ())), preferred_element_type=jnp.float32
        )
        halves = scores * (0.5 * head_dim ** (-0.5)) + bias[:, (window - count) * tok :] + seen
        weights = silu_of_half(halves).astype(jnp.bfloat16)
        out = jnp.dot(weights, values, preferred_element_type=jnp.float32)
        row = lax.broadcasted_iota(jnp.int32, (half, head_dim), 0)
        live = (block - first) * tok + core * half + row < length
        result[block] = jnp.where(live, out, 0.0).astype(jnp.bfloat16)
        landing = mix.at[chip, pl.ds(core * half, half)]

        @pl.when(me != block)
        def _():
            remote(
                result.at[block], landing, r_send.at[block], r_recv.at[me], {"seq": block}
            ).start()

        @pl.when(me == block)
        def _():
            pltpu.make_async_copy(result.at[block], landing, r_recv.at[me]).start()

    def attend_chip(other):
        for which in range(2):
            relayed = 2 * other + (1 - core)
            pltpu.make_async_copy(
                kv.at[which, relayed], kv.at[which, relayed], kv_recv.at[which, relayed]
            ).wait()
        for block in (2 * other, 2 * other + 1):
            attend(block)

    for other in range(heads):
        direct = 2 * other + core
        for which in range(2):
            landed = kv.at[which, direct]
            pltpu.make_async_copy(landed, landed, kv_recv.at[which, direct]).wait()

            @pl.when(other != chip)
            def _():
                remote(
                    landed,
                    landed,
                    fwd_send.at[which, other],
                    kv_recv.at[which, direct],
                    {"seq": sibling},
                ).start()

        if other > 0:
            attend_chip(other - 1)
    attend_chip(heads - 1)

    w_out_copy.wait()
    for source in range(n_seq):
        landing = mix.at[source // 2, pl.ds((source % 2) * half, half)]
        pltpu.make_async_copy(landing, landing, r_recv.at[source]).wait()
    mixed = jnp.concatenate([mix[head] for head in range(heads)], axis=1).astype(jnp.float32)
    gated = layer_norm(mixed) * out_gain_ref[...] * gate[...].astype(jnp.float32)
    out = jnp.dot(
        gated.astype(jnp.bfloat16), w_out_buf[...], preferred_element_type=jnp.float32
    )
    layer_rows = (x_ref[0].astype(jnp.float32) + out).astype(jnp.bfloat16)
    layer_ref[0] = layer_rows

    rows = 16
    which_user = lax.broadcasted_iota(jnp.int32, (rows, tok), 0)
    slot = lax.broadcasted_iota(jnp.int32, (rows, tok), 1) + me * tok
    last = jnp.full((rows, tok), -1, jnp.int32)
    for u in range(USERS):
        last = jnp.where(which_user == u, starts[u] * BLK + lengths[u] - 1, last)
    picker = jnp.where(slot == last, 1.0, 0.0).astype(jnp.bfloat16)
    states = jnp.dot(picker, layer_rows, preferred_element_type=jnp.float32).astype(jnp.bfloat16)
    pltpu.make_async_copy(table_ref, table_buf.at[dp], table_sem).wait()
    for step in range(1, n_dp):
        source = (dp + step) % n_dp
        pltpu.make_async_copy(
            table_buf.at[source], table_buf.at[source], table_recv.at[source]
        ).wait()
    node_scores = lax.dot_general(
        states,
        table_buf[...].reshape(n_dp * nodes, width),
        (((1,), (1,)), ((), ())),
        preferred_element_type=jnp.float32,
    )
    pieces = [
        node_scores[u : u + 1, c * LANES : (c + 1) * LANES]
        for u in range(USERS)
        for c in range(chunks)
    ]
    spare = part_sent.shape[0] - len(pieces)
    if spare:
        pieces.append(jnp.zeros((spare, LANES), jnp.float32))
    part = jnp.concatenate(pieces, axis=0).astype(jnp.bfloat16)
    part_sent[...] = part
    part_recv[me] = part
    for step in far_first(n_seq):
        copy = remote(
            part_sent,
            part_recv.at[me],
            p_send.at[step],
            p_recv.at[me],
            {"seq": (me + step) % n_seq},
        )
        copy.start()
        waits.append(copy)

    for copy in waits:
        copy.wait_send()
    for other in range(heads):
        direct = 2 * other + core

        @pl.when(other != chip)
        def _():
            for which in range(2):
                remote(
                    kv.at[which, direct],
                    kv.at[which, direct],
                    fwd_send.at[which, other],
                    kv_recv.at[which, direct],
                    {"seq": sibling},
                ).wait_send()

    for block in range(n_seq):

        @pl.when(me != block)
        def _():
            remote(
                result.at[block],
                mix.at[chip, pl.ds(core * half, half)],
                r_send.at[block],
                r_recv.at[me],
                {"seq": block},
            ).wait_send()

    for step in far_first(n_seq):
        source = (me + step) % n_seq
        pltpu.make_async_copy(
            part_recv.at[source], part_recv.at[source], p_recv.at[source]
        ).wait()
    total = jnp.sum(part_recv[...].astype(jnp.float32), axis=0)
    users = [
        jnp.concatenate(
            [total[u * chunks + c : u * chunks + c + 1] for c in range(chunks)], axis=1
        )
        for u in range(USERS)
    ]
    users.append(jnp.zeros((rows - USERS, n_dp * nodes), jnp.float32))
    score_rows = jnp.concatenate(users, axis=0).astype(jnp.bfloat16)
    picked = jnp.dot(score_rows, onehot[...], preferred_element_type=jnp.float32)
    for u in range(USERS):
        scores_ref[u : u + 1] = picked[u : u + 1, u * per_user : (u + 1) * per_user]


def body(
    n_dp,
    n_seq,
    tokens,
    in_gain,
    w_proj,
    out_gain,
    w_out,
    rab_slope,
    hist_blocks,
    hist_tail,
    node_table,
    subtree_map,
    beam_nodes,
):
    _, tok, width = tokens.shape
    heads = rab_slope.shape[0]
    head_dim = width // heads
    nodes = node_table.shape[0]
    half = tok // 2
    assert n_seq == 2 * heads and tok == BLK
    window = n_seq // 2 + 2
    part_rows = -(-USERS * n_dp * nodes // LANES // 16) * 16
    vmem = pl.BlockSpec(memory_space=pltpu.VMEM)
    smem = pl.BlockSpec(memory_space=pltpu.SMEM)
    hbm = pl.BlockSpec(memory_space=pl.ANY)
    dma = pltpu.SemaphoreType.DMA
    bf16 = jnp.bfloat16
    return pl.pallas_call(
        functools.partial(layer_kernel, n_dp, n_seq),
        out_shape=(
            jax.ShapeDtypeStruct(tokens.shape, bf16),
            jax.ShapeDtypeStruct(beam_nodes.shape, jnp.float32),
        ),
        in_specs=[vmem, vmem, hbm, vmem, hbm, smem, smem, smem, hbm, smem, vmem],
        out_specs=(vmem, vmem),
        scratch_shapes=[
            pltpu.VMEM((4, width, width), bf16),
            pltpu.VMEM((width, width), bf16),
            pltpu.VMEM((n_dp, nodes, width), bf16),
            pltpu.VMEM((3, heads, tok, head_dim), bf16),
            pltpu.VMEM((tok, width), bf16),
            pltpu.VMEM((2, n_seq, tok, head_dim), bf16),
            pltpu.VMEM((n_seq, half, head_dim), bf16),
            pltpu.VMEM((n_seq, half, head_dim), bf16),
            pltpu.VMEM((heads, tok, head_dim), bf16),
            pltpu.VMEM((half, window * tok), jnp.float32),
            pltpu.VMEM((part_rows, LANES), bf16),
            pltpu.VMEM((n_seq, part_rows, LANES), bf16),
            pltpu.VMEM((n_dp * nodes, USERS * beam_nodes.shape[1]), bf16),
            dma((4,)),
            dma,
            dma,
            dma((n_dp,)),
            dma((n_dp,)),
            dma((2, heads)),
            dma((2, n_seq)),
            dma((2, heads)),
            dma((n_seq,)),
            dma((n_seq,)),
            dma((n_seq,)),
            dma((n_seq,)),
            dma((n_seq,)),
            dma((n_seq,)),
        ],
        compiler_params=pltpu.CompilerParams(
            collective_id=0, has_side_effects=True, vmem_limit_bytes=56 * 1024 * 1024
        ),
    )(
        tokens,
        in_gain.reshape(1, width),
        w_proj,
        out_gain.reshape(1, width),
        w_out,
        rab_slope,
        hist_blocks,
        hist_tail,
        node_table,
        subtree_map,
        beam_nodes,
    )


def solution(mesh):
    placed = (
        P("dp", "seq", None),
        P(),
        P(),
        P(),
        P(),
        P(),
        P("dp", None),
        P("dp", None),
        P("dp", None),
        P(),
        P("dp", "seq"),
    )
    return jax.shard_map(
        functools.partial(body, mesh.shape["dp"], mesh.shape["seq"]),
        mesh=mesh,
        in_specs=placed,
        out_specs=(P("dp", "seq", None), P("dp", "seq")),
        check_vma=False,
    )
```

time: 174 us -> 46.6 us (0.27)
  blocking collectives: 73.7 us -> 0 us
  Pallas kernels: 0 us -> 42.9 us
  waiting for transfers between devices: 34.4 us -> 0 us
  matrix products: 21.5 us -> 0 us
  starting transfers between devices: 18 us -> 0 us
  local copies, waits for them, and re-layouts: 17.7 us -> 2.92 us
  other arithmetic: 3.57 us -> 0 us
  loops' own time: 2.72 us -> 0 us
    psum x1 -> x0, blocking collectives: 60.1 us -> none  [body(): state_rows = lax.psum(state_part, 'seq').astype(jnp.bfloat16)]
    pallas_call x0 -> x1, Pallas kernels: none -> 42.9 us  [body(): pl.pallas_call(functools.partial(layer_kernel, n_dp, n_seq), out_shape=(j...]
    all_to_all x3 -> x0, waiting for transfers between devices: 34.4 us -> none  [the longest x1 20.6 us: body(): lax.all_to_all(kv_send, 'seq', split_axis=0, concat_axis=0, tiled=True)]
    dot_general x6 -> x0, matrix products: 21.5 us -> none  [the longest x2 13.6 us: attend(): jnp.einsum('hqk,khd->qhd', weights, value_rows, preferred_element_type=jn...]
    all_to_all x3 -> x0, starting transfers between devices: 18 us -> none  [the longest x1 7.39 us: body(): lax.all_to_all(kv_send, 'seq', split_axis=0, concat_axis=0, tiled=True)]
    all_gather x2 -> x0, blocking collectives: 8.69 us -> none  [the longest x1 4.35 us: body(): lax.all_gather(state_rows, 'dp', axis=0, tiled=True)]
    gather x5 -> x0, local copies, waits for them, and re-layouts: 5.68 us -> none  [the longest x3 2.92 us: body(): jnp.take_along_axis(local_scores, jnp.clip(local_rows, 0, nodes_here - 1)...]
    unnamed x1 -> x0, blocking collectives: 4.93 us -> none
  transfers between devices with their start and end apart: 3 -> 0, of which waited for: 3 -> 0; matrix products, arithmetic and copies ran while one was open for 5% -> 0% of each run, Pallas kernels for 0% -> 0%
where the time goes in v1:
time: 46.6 us; the launch traced here: 46.4 us
  Pallas kernels  42.9 us (92%)
  local copies, waits for them, and re-layouts  2.92 us (6%)
  between operations  0.64 us (1%)
    pallas_call x1, Pallas kernels, body(): pl.pallas_call(functools.partial(layer_kernel, n_dp, n_seq), out_shape=(j...  42.9 us
    unnamed x2, local copies, waits for them, and re-layouts  2.92 us

profile of v1, /device:TPU:0, one launch (start us, length us, event | category | flops | bytes accessed | tf_op | source)
XLA Modules:
  0.0 46.4 jit_solution(4128432248045804083)
XLA Ops:
  0.6 42.9 %shard_map.122 = (bf16[1,128,1024]{2,1,0:T(8,128)(2,1)}, f32[3,64]{1,0:T(4,128)}) custom-call(bf16[1,128,1024]{2,1,0:T(8,128)(2,1)} %x_ref.1, f32[1,1024]{1,0:T(1,128)} %bitcast.2, bf16[1024,4096]{1,0:T(8,128)(2,1)} %w_proj_ref.1, f32[1,1024]{1,0:T(1,128)} %bitcast.3, bf16[1024,1024]{1,0:T(8,128)(2,1)} %w_out_ref.1, f32[8]{0:T(128)} %slope_ref.1, ...), custom_call_target="tpu_custom_call" | custom-call | tf_op jit(solution)/shard_map/pallas_call | solution.py:427
  43.5 1.7 %copy.15 = bf16[1,128,1024]{2,1,0:T(8,128)(2,1)} copy(bf16[1,128,1024]{2,1,0:T(8,128)(2,1)} %get-tuple-element.4) | data formatting | bytes 524288
  45.2 1.2 %copy.16 = f32[3,64]{1,0:T(4,128)} copy(f32[3,64]{1,0:T(4,128)} %get-tuple-element.5) | data formatting | bytes 1536

commit v2 on v1

v2 whole, which is shorter than its diff:
```python
import functools

import jax
import jax.numpy as jnp
from jax import lax
from jax.experimental import pallas as pl
from jax.experimental.pallas import tpu as pltpu
from jax.sharding import PartitionSpec as P

BLK = 128
SUBT = 64
USERS = 3
LANES = 128
MESH = pl.DeviceIdType.MESH
OFF = -1e30


def layer_norm(rows):
    centred = rows - jnp.mean(rows, axis=-1, keepdims=True)
    spread = jnp.mean(centred * centred, axis=-1, keepdims=True)
    return centred * lax.rsqrt(spread + 1e-05)


def silu_of_half(half):
    return half + half * jnp.tanh(half)


def far_first(count):
    order = []
    for step in range(count // 2):
        for offset in (count // 2 - step, count // 2 + step):
            if 0 < offset < count and offset not in order:
                order.append(offset)
    return order


def layer_kernel(
    n_dp,
    n_seq,
    x_hbm,
    in_gain_ref,
    w_proj_ref,
    out_gain_ref,
    w_out_ref,
    slope_ref,
    blocks_ref,
    tail_ref,
    table_ref,
    map_ref,
    beam_ref,
    layer_ref,
    scores_ref,
    x_ref,
    w_buf,
    w_out_buf,
    table_buf,
    sent,
    gate,
    kv,
    query,
    total_ref,
    result,
    mix,
    bias,
    part_sent,
    part_recv,
    onehot,
    x_sem,
    w_sem,
    w_out_sem,
    table_sem,
    table_send,
    table_recv,
    kv_send,
    kv_recv,
    fwd_send,
    q_send,
    q_recv,
    r_send,
    r_recv,
    p_send,
    p_recv,
):
    tok, width = x_ref.shape[1:]
    heads, _, head_dim = mix.shape
    half = query.shape[1]
    nodes = table_ref.shape[0]
    chunks = n_dp * nodes // LANES
    me = lax.axis_index("seq")
    dp = lax.axis_index("dp")
    chip, core = me // 2, me % 2
    sibling = chip * 2 + (1 - core)

    def remote(src, dst, send_sem, recv_sem, where):
        return pltpu.make_async_remote_copy(
            src_ref=src,
            dst_ref=dst,
            send_sem=send_sem,
            recv_sem=recv_sem,
            device_id=where,
            device_id_type=MESH,
        )

    bits = [(chip // (1 << bit)) % 2 for bit in range((heads - 1).bit_length())]

    def partner(step):
        return sum(
            (1 - value if step >> bit & 1 else value) * (1 << bit)
            for bit, value in enumerate(bits)
        )

    x_copy = pltpu.make_async_copy(x_hbm, x_ref, x_sem)
    x_copy.start()
    pieces = heads // 2
    pair = 2 * head_dim
    waves = ((0, pieces - 1), tuple(range(1, pieces - 1)))
    order = [(part, piece) for wave in waves for part in (2, 3, 1) for piece in wave]
    order += [(0, piece) for piece in range(pieces)]
    w_copies = {}
    for part, piece in order:
        copy = pltpu.make_async_copy(
            w_proj_ref.at[:, pl.ds(part * width + piece * pair, pair)],
            w_buf.at[part, piece],
            w_sem.at[part, piece],
        )
        copy.start()
        w_copies[part, piece] = copy

    barrier = pltpu.get_barrier_semaphore()
    for step in range(1, n_seq):
        pl.semaphore_signal(
            barrier, inc=1, device_id={"seq": (me + step) % n_seq}, device_id_type=MESH
        )
    for step in range(1, n_dp):
        pl.semaphore_signal(
            barrier, inc=1, device_id={"dp": (dp + step) % n_dp}, device_id_type=MESH
        )

    x_copy.wait()
    x_rows = x_ref[0].astype(jnp.float32)
    normed = (layer_norm(x_rows) * in_gain_ref[...]).astype(jnp.bfloat16)

    def project(part, piece):
        w_copies[part, piece].wait()
        out = jnp.dot(normed, w_buf[part, piece], preferred_element_type=jnp.float32)
        return silu_of_half(0.5 * out).astype(jnp.bfloat16)

    waits = []
    for wave in waves:
        wave_heads = [2 * piece + odd for piece in wave for odd in range(2)]
        for part in (2, 3, 1):
            slot, which = part - 1, part - 2
            for piece in wave:
                rows = project(part, piece)
                sent[slot, 2 * piece] = rows[:, :head_dim]
                sent[slot, 2 * piece + 1] = rows[:, head_dim:]
            if part == 2 and wave is waves[0]:
                pl.semaphore_wait(barrier, n_seq - 1 + n_dp - 1)
            for head in wave_heads:
                for core_to in range(2):
                    if part == 1:
                        piece_ref = sent.at[0, head, pl.ds(core_to * half, half)]
                        landing, send_sem, recv_sem = query.at[me], q_send, q_recv.at[me]
                        goes = True
                    else:
                        piece_ref, landing = sent.at[slot, head], kv.at[which, me]
                        send_sem, recv_sem = kv_send.at[which], kv_recv.at[which, me]
                        goes = (chip == head) | (core == core_to)
                    here = me == 2 * head + core_to

                    @pl.when(jnp.logical_not(here) & goes)
                    def _():
                        remote(
                            piece_ref,
                            landing,
                            send_sem.at[2 * head + core_to],
                            recv_sem,
                            {"seq": 2 * head + core_to},
                        ).start()

                    @pl.when(here)
                    def _():
                        pltpu.make_async_copy(piece_ref, landing, recv_sem).start()

    for step in range(1, n_dp):
        copy = remote(
            table_ref,
            table_buf.at[dp],
            table_send.at[step],
            table_recv.at[dp],
            {"dp": (dp + step) % n_dp},
        )
        copy.start()
        waits.append(copy)
    pltpu.make_async_copy(table_ref, table_buf.at[dp], table_sem).start()
    w_out_copy = pltpu.make_async_copy(w_out_ref, w_out_buf, w_out_sem)
    w_out_copy.start()

    for piece in range(pieces):
        gate[:, piece * pair : (piece + 1) * pair] = project(0, piece)

    row = lax.broadcasted_iota(jnp.int32, bias.shape, 0)
    column = lax.broadcasted_iota(jnp.int32, bias.shape, 1)
    gap = (row // half) * tok + row % half + core * half - column
    slope = slope_ref[chip]
    logs = jnp.log(1.0 + jnp.maximum(gap, 0).astype(jnp.float32))
    bias[...] = jnp.where(gap >= 0, (0.5 * slope) * logs, OFF)
    total_ref[...] = jnp.zeros_like(total_ref)
    query[n_seq:] = jnp.zeros((query.shape[0] - n_seq, half, head_dim), jnp.bfloat16)

    beams = beam_ref[...]
    subtree = beams >> 6
    base = jnp.zeros_like(beams)
    for index in range(map_ref.shape[0]):
        base = jnp.where(subtree == index, map_ref[index], base)
    stored = base * SUBT + (beams & (SUBT - 1))
    per_user = beams.shape[1]
    stored_row = jnp.concatenate([stored[u : u + 1] for u in range(USERS)], axis=1)
    node = lax.broadcasted_iota(jnp.int32, onehot.shape, 0)
    onehot[...] = jnp.where(node == stored_row, 1.0, 0.0).astype(jnp.bfloat16)

    starts = [0, blocks_ref[0, 0], blocks_ref[0, 0] + blocks_ref[0, 1]]
    lengths = [(blocks_ref[0, u] - 1) * BLK + tail_ref[0, u] for u in range(USERS)]

    def owner(block):
        first = jnp.where(block >= starts[1], starts[1], 0)
        length = jnp.where(block >= starts[1], lengths[1], lengths[0])
        first = jnp.where(block >= starts[2], starts[2], first)
        length = jnp.where(block >= starts[2], lengths[2], length)
        return first, length

    def landed(ref, sem):
        pltpu.make_async_copy(ref, ref, sem).wait()

    span = bias.shape[0] // half
    key_block = lax.broadcasted_iota(jnp.int32, (1, 2 * tok), 1) // tok

    def attend(other):
        block = 2 * other
        queries = query[pl.ds(block, span)].reshape(span * half, head_dim)
        keys = kv[0, pl.ds(block, 2)].reshape(2 * tok, head_dim)
        values = kv[1, pl.ds(block, 2)].reshape(2 * tok, head_dim)
        scores = lax.dot_general(
            queries, keys, (((1,), (1,)), ((), ())), preferred_element_type=jnp.float32
        )
        weights = []
        for ahead in range(span):
            first, _ = owner(block + ahead)
            seen = jnp.where(key_block + block >= first, 0.0, OFF)
            rows = slice(ahead * half, (ahead + 1) * half)
            halves = scores[rows] * (0.5 * head_dim ** (-0.5)) + bias[rows] + seen
            weights.append(silu_of_half(halves).astype(jnp.bfloat16))
        out = jnp.dot(
            jnp.concatenate(weights, axis=0), values, preferred_element_type=jnp.float32
        )
        total_ref[pl.ds(block, span)] += out.reshape(span, half, head_dim)

    def relay(step):
        other = partner(step)
        for which in range(2):
            ref = kv.at[which, 2 * other + core]
            sem = kv_recv.at[which, 2 * other + core]
            landed(ref, sem)
            if step > 0:
                copy = remote(ref, ref, fwd_send.at[which, step], sem, {"seq": sibling})
                copy.start()
                waits.append(copy)

    def attend_relayed(step):
        other = partner(step)
        for which in range(2):
            block = 2 * other + (1 - core)
            landed(kv.at[which, block], kv_recv.at[which, block])
        attend(other)

    relay(0)
    for step in range(1, heads):
        relay(step)
        if step == 1:
            for block in range(n_seq):
                landed(query.at[block], q_recv.at[block])
        attend_relayed(step - 1)
    attend_relayed(heads - 1)

    row = lax.broadcasted_iota(jnp.int32, (half, head_dim), 0)
    landing = mix.at[chip, pl.ds(core * half, half)]
    for step in reversed(range(heads)):
        for part in range(2):
            block = 2 * partner(step) + (core if part == 0 else 1 - core)
            first, length = owner(block)
            live = (block - first) * tok + core * half + row < length
            result[block] = jnp.where(live, total_ref[block], 0.0).astype(jnp.bfloat16)
            if step == 0 and part == 0:
                pltpu.make_async_copy(result.at[block], landing, r_recv.at[me]).start()
            else:
                copy = remote(
                    result.at[block],
                    landing,
                    r_send.at[2 * step + part],
                    r_recv.at[me],
                    {"seq": block},
                )
                copy.start()
                waits.append(copy)

    w_out_copy.wait()
    for source in range(n_seq):
        landing = mix.at[source // 2, pl.ds((source % 2) * half, half)]
        pltpu.make_async_copy(landing, landing, r_recv.at[source]).wait()
    mixed = jnp.concatenate([mix[head] for head in range(heads)], axis=1).astype(jnp.float32)
    gated = layer_norm(mixed) * out_gain_ref[...] * gate[...].astype(jnp.float32)
    out = jnp.dot(
        gated.astype(jnp.bfloat16), w_out_buf[...], preferred_element_type=jnp.float32
    )
    layer_rows = (x_ref[0].astype(jnp.float32) + out).astype(jnp.bfloat16)

    rows = 16
    which_user = lax.broadcasted_iota(jnp.int32, (rows, tok), 0)
    slot = lax.broadcasted_iota(jnp.int32, (rows, tok), 1) + me * tok
    last = jnp.full((rows, tok), -1, jnp.int32)
    for u in range(USERS):
        last = jnp.where(which_user == u, starts[u] * BLK + lengths[u] - 1, last)
    picker = jnp.where(slot == last, 1.0, 0.0).astype(jnp.bfloat16)
    states = jnp.dot(picker, layer_rows, preferred_element_type=jnp.float32).astype(jnp.bfloat16)
    pltpu.make_async_copy(table_ref, table_buf.at[dp], table_sem).wait()
    for step in range(1, n_dp):
        source = (dp + step) % n_dp
        pltpu.make_async_copy(
            table_buf.at[source], table_buf.at[source], table_recv.at[source]
        ).wait()
    node_scores = lax.dot_general(
        states,
        table_buf[...].reshape(n_dp * nodes, width),
        (((1,), (1,)), ((), ())),
        preferred_element_type=jnp.float32,
    )
    pieces = [
        node_scores[u : u + 1, c * LANES : (c + 1) * LANES]
        for u in range(USERS)
        for c in range(chunks)
    ]
    spare = part_sent.shape[0] - len(pieces)
    if spare:
        pieces.append(jnp.zeros((spare, LANES), jnp.float32))
    part = jnp.concatenate(pieces, axis=0).astype(jnp.bfloat16)
    part_sent[...] = part
    part_recv[me] = part
    for step in far_first(n_seq):
        copy = remote(
            part_sent,
            part_recv.at[me],
            p_send.at[step],
            p_recv.at[me],
            {"seq": (me + step) % n_seq},
        )
        copy.start()
        waits.append(copy)

    layer_ref[0] = layer_rows

    for copy in waits:
        copy.wait_send()
    for head in range(heads):
        for core_to in range(2):
            away = me != 2 * head + core_to
            where = {"seq": 2 * head + core_to}

            @pl.when(away)
            def _():
                remote(
                    sent.at[0, head, pl.ds(core_to * half, half)],
                    query.at[me],
                    q_send.at[2 * head + core_to],
                    q_recv.at[me],
                    where,
                ).wait_send()

            @pl.when(away & ((chip == head) | (core == core_to)))
            def _():
                for which in range(2):
                    remote(
                        sent.at[which + 1, head],
                        kv.at[which, me],
                        kv_send.at[which, 2 * head + core_to],
                        kv_recv.at[which, me],
                        where,
                    ).wait_send()

    for step in far_first(n_seq):
        source = (me + step) % n_seq
        pltpu.make_async_copy(
            part_recv.at[source], part_recv.at[source], p_recv.at[source]
        ).wait()
    total = jnp.sum(part_recv[...].astype(jnp.float32), axis=0)
    users = [
        jnp.concatenate(
            [total[u * chunks + c : u * chunks + c + 1] for c in range(chunks)], axis=1
        )
        for u in range(USERS)
    ]
    users.append(jnp.zeros((rows - USERS, n_dp * nodes), jnp.float32))
    score_rows = jnp.concatenate(users, axis=0).astype(jnp.bfloat16)
    picked = jnp.dot(score_rows, onehot[...], preferred_element_type=jnp.float32)
    for u in range(USERS):
        scores_ref[u : u + 1] = picked[u : u + 1, u * per_user : (u + 1) * per_user]


def hand_over(layer_in, scores_in, layer_out, scores_out, layer_sem, scores_sem):
    layer = pltpu.make_async_copy(layer_in, layer_out, layer_sem)
    scores = pltpu.make_async_copy(scores_in, scores_out, scores_sem)
    layer.start()
    scores.start()
    layer.wait()
    scores.wait()


def body(
    n_dp,
    n_seq,
    tokens,
    in_gain,
    w_proj,
    out_gain,
    w_out,
    rab_slope,
    hist_blocks,
    hist_tail,
    node_table,
    subtree_map,
    beam_nodes,
):
    _, tok, width = tokens.shape
    heads = rab_slope.shape[0]
    head_dim = width // heads
    nodes = node_table.shape[0]
    half = tok // 2
    assert n_seq == 2 * heads and tok == BLK
    window = n_seq // 2 + 2
    part_rows = -(-USERS * n_dp * nodes // LANES // 16) * 16
    vmem = pl.BlockSpec(memory_space=pltpu.VMEM)
    smem = pl.BlockSpec(memory_space=pltpu.SMEM)
    hbm = pl.BlockSpec(memory_space=pl.ANY)
    dma = pltpu.SemaphoreType.DMA
    bf16 = jnp.bfloat16
    layer_out, scores = pl.pallas_call(
        functools.partial(layer_kernel, n_dp, n_seq),
        out_shape=(
            jax.ShapeDtypeStruct(tokens.shape, bf16),
            jax.ShapeDtypeStruct(beam_nodes.shape, jnp.float32),
        ),
        in_specs=[hbm, vmem, hbm, vmem, hbm, smem, smem, smem, hbm, smem, vmem],
        out_specs=(vmem, vmem),
        scratch_shapes=[
            pltpu.VMEM(tokens.shape, bf16),
            pltpu.VMEM((4, heads // 2, width, 2 * head_dim), bf16),
            pltpu.VMEM((width, width), bf16),
            pltpu.VMEM((n_dp, nodes, width), bf16),
            pltpu.VMEM((3, heads, tok, head_dim), bf16),
            pltpu.VMEM((tok, width), bf16),
            pltpu.VMEM((2, n_seq, tok, head_dim), bf16),
            pltpu.VMEM((n_seq + window, half, head_dim), bf16),
            pltpu.VMEM((n_seq + window, half, head_dim), jnp.float32),
            pltpu.VMEM((n_seq, half, head_dim), bf16),
            pltpu.VMEM((heads, tok, head_dim), bf16),
            pltpu.VMEM(((window + 1) * half, 2 * tok), jnp.float32),
            pltpu.VMEM((part_rows, LANES), bf16),
            pltpu.VMEM((n_seq, part_rows, LANES), bf16),
            pltpu.VMEM((n_dp * nodes, USERS * beam_nodes.shape[1]), bf16),
            dma,
            dma((4, heads // 2)),
            dma,
            dma,
            dma((n_dp,)),
            dma((n_dp,)),
            dma((2, n_seq)),
            dma((2, n_seq)),
            dma((2, heads)),
            dma((n_seq,)),
            dma((n_seq,)),
            dma((n_seq,)),
            dma((n_seq,)),
            dma((n_seq,)),
            dma((n_seq,)),
        ],
        compiler_params=pltpu.CompilerParams(
            collective_id=0, has_side_effects=True, vmem_limit_bytes=56 * 1024 * 1024
        ),
    )(
        tokens,
        in_gain.reshape(1, width),
        w_proj,
        out_gain.reshape(1, width),
        w_out,
        rab_slope,
        hist_blocks,
        hist_tail,
        node_table,
        subtree_map,
        beam_nodes,
    )
    return pl.pallas_call(
        hand_over,
        out_shape=(
            jax.ShapeDtypeStruct(layer_out.shape, bf16),
            jax.ShapeDtypeStruct(scores.shape, jnp.float32),
        ),
        in_specs=[pl.BlockSpec(memory_space=pltpu.HBM)] * 2,
        out_specs=(pl.BlockSpec(memory_space=pltpu.HBM),) * 2,
        scratch_shapes=[dma, dma],
        compiler_params=pltpu.CompilerParams(vmem_limit_bytes=56 * 1024 * 1024),
    )(layer_out, scores)


def solution(mesh):
    placed = (
        P("dp", "seq", None),
        P(),
        P(),
        P(),
        P(),
        P(),
        P("dp", None),
        P("dp", None),
        P("dp", None),
        P(),
        P("dp", "seq"),
    )
    return jax.shard_map(
        functools.partial(body, mesh.shape["dp"], mesh.shape["seq"]),
        mesh=mesh,
        in_specs=placed,
        out_specs=(P("dp", "seq", None), P("dp", "seq")),
        check_vma=False,
    )
```

time: 46.6 us -> 55.5 us (1.19)
  Pallas kernels: 42.9 us -> 54.6 us
  local copies, waits for them, and re-layouts: 2.92 us -> 0 us
    pallas_call x0 -> x1, Pallas kernels: none -> 9.11 us  [body(): pl.pallas_call(hand_over, out_shape=(jax.ShapeDtypeStruct(layer_out.shape...]
    unnamed x2 -> x0, local copies, waits for them, and re-layouts: 2.92 us -> none
    pallas_call x1, Pallas kernels: 42.9 us -> 45.5 us  [body(): pl.pallas_call(functools.partial(layer_kernel, n_dp, n_seq), out_shape=(j...]
where the time goes in v2:
time: 55.5 us; the launch traced here: 55.3 us
  Pallas kernels  54.6 us (98%)
  between operations  0.64 us (1%)
    pallas_call x1, Pallas kernels, body(): pl.pallas_call(functools.partial(layer_kernel, n_dp, n_seq), out_shape=(j...  45.5 us
    pallas_call x1, Pallas kernels, body(): pl.pallas_call(hand_over, out_shape=(jax.ShapeDtypeStruct(layer_out.shape...  9.11 us

profile of v2, /device:TPU:0, one launch (start us, length us, event | category | flops | bytes accessed | tf_op | source)
XLA Modules:
  0.0 55.3 jit_solution(3633349693088850924)
XLA Ops:
  0.6 45.5 %shard_map.122 = (bf16[1,128,1024]{2,1,0:T(8,128)(2,1)}, f32[3,64]{1,0:T(4,128)}) custom-call(bf16[1,128,1024]{2,1,0:T(8,128)(2,1)} %x_hbm.1, f32[1,1024]{1,0:T(1,128)} %bitcast.2, bf16[1024,4096]{1,0:T(8,128)(2,1)} %w_proj_ref.1, f32[1,1024]{1,0:T(1,128)} %bitcast.3, bf16[1024,1024]{1,0:T(8,128)(2,1)} %w_out_ref.1, f32[8]{0:T(128)} %slope_ref.1, ...), custom_call_target="tpu_custom_call" | custom-call | tf_op jit(solution)/shard_map/pallas_call | solution.py:445
  46.2 9.1 %shard_map.123 = (bf16[1,128,1024]{2,1,0:T(8,128)(2,1)}, f32[3,64]{1,0:T(4,128)}) custom-call(bf16[1,128,1024]{2,1,0:T(8,128)(2,1)} %get-tuple-element.4.layer_in, f32[3,64]{1,0:T(4,128)} %get-tuple-element.5.scores_in), custom_call_target="tpu_custom_call" | custom-call | tf_op jit(solution)/shard_map/pallas_call | solution.py:501

commit v3 on v1

--- a/solution.py
+++ b/solution.py
@@ -37,7 +37,7 @@
 def layer_kernel(
     n_dp,
     n_seq,
-    x_ref,
+    x_hbm,
     in_gain_ref,
     w_proj_ref,
     out_gain_ref,
@@ -50,6 +50,7 @@
     beam_ref,
     layer_ref,
     scores_ref,
+    x_ref,
     w_buf,
     w_out_buf,
     table_buf,
@@ -63,11 +64,14 @@
     part_sent,
     part_recv,
     onehot,
+    x_sem,
     w_sem,
     w_out_sem,
     table_sem,
     table_send,
     table_recv,
+    table_fwd,
+    table_relay,
     kv_send,
     kv_recv,
     fwd_send,
@@ -99,6 +103,8 @@
             device_id_type=MESH,
         )
 
+    x_copy = pltpu.make_async_copy(x_hbm, x_ref, x_sem)
+    x_copy.start()
     order = (2, 3, 1, 0)
     w_copies = {
         part: pltpu.make_async_copy(
@@ -119,6 +125,7 @@
             barrier, inc=1, device_id={"dp": (dp + step) % n_dp}, device_id_type=MESH
         )
 
+    x_copy.wait()
     x_rows = x_ref[0].astype(jnp.float32)
     normed = (layer_norm(x_rows) * in_gain_ref[...]).astype(jnp.bfloat16)
 
@@ -138,11 +145,24 @@
 
     chip_order = far_first(heads)
     waits = []
+    pl.semaphore_wait(barrier, n_seq - 1 + n_dp - 1)
+
+    part_nodes = nodes // 2
+    for step in range(1, n_dp):
+        mine = pl.ds(core * part_nodes, part_nodes)
+        copy = remote(
+            table_ref.at[mine],
+            table_buf.at[dp, mine],
+            table_send.at[step],
+            table_recv.at[dp],
+            {"dp": (dp + step) % n_dp},
+        )
+        copy.start()
+        waits.append(copy)
+    pltpu.make_async_copy(table_ref, table_buf.at[dp], table_sem).start()
     for which in range(2):
         slot = which + 1
         project(slot + 1, store_heads(slot))
-        if which == 0:
-            pl.semaphore_wait(barrier, n_seq - 1 + n_dp - 1)
         for step in chip_order:
             head = (chip + step) % heads
             copy = remote(
@@ -193,17 +213,6 @@
         sent.at[0, chip, pl.ds(core * half, half)], query.at[me], q_recv.at[me]
     ).start()
 
-    for step in range(1, n_dp):
-        copy = remote(
-            table_ref,
-            table_buf.at[dp],
-            table_send.at[step],
-            table_recv.at[dp],
-            {"dp": (dp + step) % n_dp},
-        )
-        copy.start()
-        waits.append(copy)
-    pltpu.make_async_copy(table_ref, table_buf.at[dp], table_sem).start()
     w_out_copy = pltpu.make_async_copy(w_out_ref, w_out_buf, w_out_sem)
     w_out_copy.start()
 
@@ -293,6 +302,13 @@
 
         if other > 0:
             attend_chip(other - 1)
+    for step in range(1, n_dp):
+        source = (dp + step) % n_dp
+        came = table_buf.at[source, pl.ds(core * part_nodes, part_nodes)]
+        pltpu.make_async_copy(came, came, table_recv.at[source]).wait()
+        copy = remote(came, came, table_fwd.at[step], table_relay.at[source], {"seq": sibling})
+        copy.start()
+        waits.append(copy)
     attend_chip(heads - 1)
 
     w_out_copy.wait()
@@ -305,7 +321,6 @@
         gated.astype(jnp.bfloat16), w_out_buf[...], preferred_element_type=jnp.float32
     )
     layer_rows = (x_ref[0].astype(jnp.float32) + out).astype(jnp.bfloat16)
-    layer_ref[0] = layer_rows
 
     rows = 16
     which_user = lax.broadcasted_iota(jnp.int32, (rows, tok), 0)
@@ -318,9 +333,8 @@
     pltpu.make_async_copy(table_ref, table_buf.at[dp], table_sem).wait()
     for step in range(1, n_dp):
         source = (dp + step) % n_dp
-        pltpu.make_async_copy(
-            table_buf.at[source], table_buf.at[source], table_recv.at[source]
-        ).wait()
+        came = table_buf.at[source, pl.ds((1 - core) * part_nodes, part_nodes)]
+        pltpu.make_async_copy(came, came, table_relay.at[source]).wait()
     node_scores = lax.dot_general(
         states,
         table_buf[...].reshape(n_dp * nodes, width),
@@ -349,6 +363,8 @@
         copy.start()
         waits.append(copy)
 
+    layer_ref[0] = layer_rows
+
     for copy in waits:
         copy.wait_send()
     for other in range(heads):
@@ -394,6 +410,15 @@
     picked = jnp.dot(score_rows, onehot[...], preferred_element_type=jnp.float32)
     for u in range(USERS):
         scores_ref[u : u + 1] = picked[u : u + 1, u * per_user : (u + 1) * per_user]
+
+
+def hand_over(layer_in, scores_in, layer_out, scores_out, layer_sem, scores_sem):
+    layer = pltpu.make_async_copy(layer_in, layer_out, layer_sem)
+    scores = pltpu.make_async_copy(scores_in, scores_out, scores_sem)
+    layer.start()
+    scores.start()
+    layer.wait()
+    scores.wait()
 
 
 def body(
@@ -424,15 +449,16 @@
     hbm = pl.BlockSpec(memory_space=pl.ANY)
     dma = pltpu.SemaphoreType.DMA
     bf16 = jnp.bfloat16
-    return pl.pallas_call(
+    layer_out, scores = pl.pallas_call(
         functools.partial(layer_kernel, n_dp, n_seq),
         out_shape=(
             jax.ShapeDtypeStruct(tokens.shape, bf16),
             jax.ShapeDtypeStruct(beam_nodes.shape, jnp.float32),
         ),
-        in_specs=[vmem, vmem, hbm, vmem, hbm, smem, smem, smem, hbm, smem, vmem],
+        in_specs=[hbm, vmem, hbm, vmem, hbm, smem, smem, smem, hbm, smem, vmem],
         out_specs=(vmem, vmem),
         scratch_shapes=[
+            pltpu.VMEM(tokens.shape, bf16),
             pltpu.VMEM((4, width, width), bf16),
             pltpu.VMEM((width, width), bf16),
             pltpu.VMEM((n_dp, nodes, width), bf16),
@@ -446,9 +472,12 @@
             pltpu.VMEM((part_rows, LANES), bf16),
             pltpu.VMEM((n_seq, part_rows, LANES), bf16),
             pltpu.VMEM((n_dp * nodes, USERS * beam_nodes.shape[1]), bf16),
+            dma,
             dma((4,)),
             dma,
             dma,
+            dma((n_dp,)),
+            dma((n_dp,)),
             dma((n_dp,)),
             dma((n_dp,)),
             dma((2, heads)),
@@ -477,6 +506,16 @@
         subtree_map,
         beam_nodes,
     )
+    return pl.pallas_call(
+        hand_over,
+        out_shape=(
+            jax.ShapeDtypeStruct(layer_out.shape, bf16),
+            jax.ShapeDtypeStruct(scores.shape, jnp.float32),
+        ),
+        in_specs=[vmem, vmem],
+        out_specs=(hbm, hbm),
+        scratch_shapes=[dma, dma],
+    )(layer_out, scores)
 
 
 def solution(mesh):

time: 46.6 us -> 46.7 us (level)
  Pallas kernels: 42.9 us -> 45.9 us
  local copies, waits for them, and re-layouts: 2.92 us -> 0 us
    unnamed x2 -> x0, local copies, waits for them, and re-layouts: 2.92 us -> none
    pallas_call x0 -> x1, Pallas kernels: none -> 1.67 us  [body(): pl.pallas_call(hand_over, out_shape=(jax.ShapeDtypeStruct(layer_out.shape...]
    pallas_call x1, Pallas kernels: 42.9 us -> 44.2 us  [body(): pl.pallas_call(functools.partial(layer_kernel, n_dp, n_seq), out_shape=(j...]
where the time goes in v3:
time: 46.7 us; the launch traced here: 46.6 us
  Pallas kernels  45.9 us (98%)
  between operations  0.64 us (1%)
    pallas_call x1, Pallas kernels, body(): pl.pallas_call(functools.partial(layer_kernel, n_dp, n_seq), out_shape=(j...  44.2 us
    pallas_call x1, Pallas kernels, body(): pl.pallas_call(hand_over, out_shape=(jax.ShapeDtypeStruct(layer_out.shape...  1.67 us

profile of v3, /device:TPU:0, one launch (start us, length us, event | category | flops | bytes accessed | tf_op | source)
XLA Modules:
  0.0 46.6 jit_solution(7826130922381900190)
XLA Ops:
  0.6 44.2 %shard_map.122 = (bf16[1,128,1024]{2,1,0:T(8,128)(2,1)}, f32[3,64]{1,0:T(4,128)}) custom-call(bf16[1,128,1024]{2,1,0:T(8,128)(2,1)} %x_hbm.1, f32[1,1024]{1,0:T(1,128)} %bitcast.2, bf16[1024,4096]{1,0:T(8,128)(2,1)} %w_proj_ref.1, f32[1,1024]{1,0:T(1,128)} %bitcast.3, bf16[1024,1024]{1,0:T(8,128)(2,1)} %w_out_ref.1, f32[8]{0:T(128)} %slope_ref.1, ...), custom_call_target="tpu_custom_call" | custom-call | tf_op jit(solution)/shard_map/pallas_call | solution.py:452
  44.9 1.7 %shard_map.123 = (bf16[1,128,1024]{2,1,0:T(8,128)(2,1)}, f32[3,64]{1,0:T(4,128)}) custom-call(bf16[1,128,1024]{2,1,0:T(8,128)(2,1)} %get-tuple-element.4.layer_in, f32[3,64]{1,0:T(4,128)} %get-tuple-element.5.scores_in), custom_call_target="tpu_custom_call" | custom-call | tf_op jit(solution)/shard_map/pallas_call | solution.py:509

commit v4 on v3

--- a/solution.py
+++ b/solution.py
@@ -60,6 +60,7 @@
     query,
     result,
     mix,
+    mix_low,
     bias,
     part_sent,
     part_recv,
@@ -74,24 +75,25 @@
     table_relay,
     kv_send,
     kv_recv,
-    fwd_send,
     q_send,
+    cross_send,
     q_recv,
     r_send,
     r_recv,
+    r_low_recv,
     p_send,
     p_recv,
 ):
     tok, width = x_ref.shape[1:]
     heads, _, head_dim = mix.shape
-    half = query.shape[1]
-    window = bias.shape[1] // tok
     nodes = table_ref.shape[0]
     chunks = n_dp * nodes // LANES
     me = lax.axis_index("seq")
     dp = lax.axis_index("dp")
-    chip, core = me // 2, me % 2
-    sibling = chip * 2 + (1 - core)
+    side, mine = me // heads, me % heads
+    base = side * heads
+    core = me % 2
+    sibling = me + 1 - 2 * core
 
     def remote(src, dst, send_sem, recv_sem, where):
         return pltpu.make_async_remote_copy(
@@ -105,7 +107,7 @@
 
     x_copy = pltpu.make_async_copy(x_hbm, x_ref, x_sem)
     x_copy.start()
-    order = (2, 3, 1, 0)
+    order = (1, 2, 3, 0)
     w_copies = {
         part: pltpu.make_async_copy(
             w_proj_ref.at[:, pl.ds(part * width, width)], w_buf.at[part], w_sem.at[part]
@@ -143,16 +145,44 @@
 
         return store
 
-    chip_order = far_first(heads)
     waits = []
-    pl.semaphore_wait(barrier, n_seq - 1 + n_dp - 1)
+    for slot, landing, send_sem, recv_sem in (
+        (0, query.at[me], q_send, q_recv.at[me]),
+        (1, kv.at[0, mine], kv_send.at[0], kv_recv.at[0, mine]),
+        (2, kv.at[1, mine], kv_send.at[1], kv_recv.at[1, mine]),
+    ):
+        project(slot + 1, store_heads(slot))
+        if slot == 0:
+            pl.semaphore_wait(barrier, n_seq - 1 + n_dp - 1)
+        for step in range(heads):
+            head = (mine + step) % heads
+            if slot == 0:
+
+                @pl.when(side == 1)
+                def _():
+                    remote(
+                        sent.at[0, head],
+                        query.at[me],
+                        cross_send.at[step],
+                        q_recv.at[me],
+                        {"seq": head},
+                    ).start()
+
+            if step == 0:
+                pltpu.make_async_copy(sent.at[slot, head], landing, recv_sem).start()
+            else:
+                copy = remote(
+                    sent.at[slot, head], landing, send_sem.at[step], recv_sem, {"seq": base + head}
+                )
+                copy.start()
+                waits.append(copy)
 
     part_nodes = nodes // 2
     for step in range(1, n_dp):
-        mine = pl.ds(core * part_nodes, part_nodes)
+        own_rows = pl.ds(core * part_nodes, part_nodes)
         copy = remote(
-            table_ref.at[mine],
-            table_buf.at[dp, mine],
+            table_ref.at[own_rows],
+            table_buf.at[dp, own_rows],
             table_send.at[step],
             table_recv.at[dp],
             {"dp": (dp + step) % n_dp},
@@ -160,59 +190,6 @@
         copy.start()
         waits.append(copy)
     pltpu.make_async_copy(table_ref, table_buf.at[dp], table_sem).start()
-    for which in range(2):
-        slot = which + 1
-        project(slot + 1, store_heads(slot))
-        for step in chip_order:
-            head = (chip + step) % heads
-            copy = remote(
-                sent.at[slot, head],
-                kv.at[which, me],
-                kv_send.at[which, step],
-                kv_recv.at[which, me],
-                {"seq": head * 2 + core},
-            )
-            copy.start()
-            waits.append(copy)
-        copy = remote(
-            sent.at[slot, chip],
-            kv.at[which, me],
-            kv_send.at[which, 0],
-            kv_recv.at[which, me],
-            {"seq": sibling},
-        )
-        copy.start()
-        waits.append(copy)
-        pltpu.make_async_copy(
-            sent.at[slot, chip], kv.at[which, me], kv_recv.at[which, me]
-        ).start()
-
-    project(1, store_heads(0))
-    for step in chip_order:
-        head = (chip + step) % heads
-        for part in range(2):
-            copy = remote(
-                sent.at[0, head, pl.ds(part * half, half)],
-                query.at[me],
-                q_send.at[2 * step + part],
-                q_recv.at[me],
-                {"seq": head * 2 + part},
-            )
-            copy.start()
-            waits.append(copy)
-    copy = remote(
-        sent.at[0, chip, pl.ds((1 - core) * half, half)],
-        query.at[me],
-        q_send.at[0],
-        q_recv.at[me],
-        {"seq": sibling},
-    )
-    copy.start()
-    waits.append(copy)
-    pltpu.make_async_copy(
-        sent.at[0, chip, pl.ds(core * half, half)], query.at[me], q_recv.at[me]
-    ).start()
-
     w_out_copy = pltpu.make_async_copy(w_out_ref, w_out_buf, w_out_sem)
     w_out_copy.start()
 
@@ -223,17 +200,21 @@
 
     row = lax.broadcasted_iota(jnp.int32, bias.shape, 0)
     column = lax.broadcasted_iota(jnp.int32, bias.shape, 1)
-    gap = (window - 1) * tok + core * half + row - column
-    slope = slope_ref[chip]
+    gap = (n_seq - 1) * tok + row - column
+    slope = slope_ref[mine]
     logs = jnp.log(1.0 + jnp.maximum(gap, 0).astype(jnp.float32))
     bias[...] = jnp.where(gap >= 0, (0.5 * slope) * logs, OFF)
 
+    @pl.when(side == 0)
+    def _():
+        mix_low[...] = jnp.zeros_like(mix_low)
+
     beams = beam_ref[...]
     subtree = beams >> 6
-    base = jnp.zeros_like(beams)
+    found = jnp.zeros_like(beams)
     for index in range(map_ref.shape[0]):
-        base = jnp.where(subtree == index, map_ref[index], base)
-    stored = base * SUBT + (beams & (SUBT - 1))
+        found = jnp.where(subtree == index, map_ref[index], found)
+    stored = found * SUBT + (beams & (SUBT - 1))
     per_user = beams.shape[1]
     stored_row = jnp.concatenate([stored[u : u + 1] for u in range(USERS)], axis=1)
     node = lax.broadcasted_iota(jnp.int32, onehot.shape, 0)
@@ -242,80 +223,103 @@
     starts = [0, blocks_ref[0, 0], blocks_ref[0, 0] + blocks_ref[0, 1]]
     lengths = [(blocks_ref[0, u] - 1) * BLK + tail_ref[0, u] for u in range(USERS)]
 
-    def attend(block):
-        pltpu.make_async_copy(query.at[block], query.at[block], q_recv.at[block]).wait()
-        count = min(block + 1, window)
-        low = block + 1 - count
-        keys = kv[0, low : block + 1].reshape(count * tok, head_dim)
-        values = kv[1, low : block + 1].reshape(count * tok, head_dim)
+    def landed(ref, sem):
+        pltpu.make_async_copy(ref, ref, sem).wait()
+
+    def attend(block, first_key, key_rows, value_rows, bias_rows):
         first = jnp.where(block >= starts[1], starts[1], 0)
         length = jnp.where(block >= starts[1], lengths[1], lengths[0])
         first = jnp.where(block >= starts[2], starts[2], first)
         length = jnp.where(block >= starts[2], lengths[2], length)
-        column = lax.broadcasted_iota(jnp.int32, (1, count * tok), 1) + low * tok
+        column = lax.broadcasted_iota(jnp.int32, (1, key_rows.shape[0]), 1) + first_key * tok
         seen = jnp.where(column >= first * tok, 0.0, OFF)
         scores = lax.dot_general(
-            query[block], keys, (((1,), (1,)), ((), ())), preferred_element_type=jnp.float32
-        )
-        halves = scores * (0.5 * head_dim ** (-0.5)) + bias[:, (window - count) * tok :] + seen
+            query[block], key_rows, (((1,), (1,)), ((), ())), preferred_element_type=jnp.float32
+        )
+        halves = scores * (0.5 * head_dim ** (-0.5)) + bias_rows + seen
         weights = silu_of_half(halves).astype(jnp.bfloat16)
-        out = jnp.dot(weights, values, preferred_element_type=jnp.float32)
-        row = lax.broadcasted_iota(jnp.int32, (half, head_dim), 0)
-        live = (block - first) * tok + core * half + row < length
-        result[block] = jnp.where(live, out, 0.0).astype(jnp.bfloat16)
-        landing = mix.at[chip, pl.ds(core * half, half)]
-
-        @pl.when(me != block)
+        out = jnp.dot(weights, value_rows, preferred_element_type=jnp.float32)
+        row = lax.broadcasted_iota(jnp.int32, (tok, head_dim), 0)
+        live = (block - first) * tok + row < length
+        return jnp.where(live, out, 0.0).astype(jnp.bfloat16)
+
+    def key_values(which, count):
+        return kv[which, 0:count].reshape(count * tok, head_dim)
+
+    for place in range(heads):
+        block = base + place
+        landed(query.at[block], q_recv.at[block])
+        for which in range(2):
+            landed(kv.at[which, place], kv_recv.at[which, place])
+        count = place + 1
+        result[place] = attend(
+            block,
+            base,
+            key_values(0, count),
+            key_values(1, count),
+            bias[:, (n_seq - count) * tok :],
+        )
+
+        @pl.when(mine != place)
         def _():
             remote(
-                result.at[block], landing, r_send.at[block], r_recv.at[me], {"seq": block}
+                result.at[place], mix.at[mine], r_send.at[place], r_recv.at[mine], {"seq": block}
             ).start()
 
-        @pl.when(me == block)
+        @pl.when(mine == place)
         def _():
-            pltpu.make_async_copy(result.at[block], landing, r_recv.at[me]).start()
-
-    def attend_chip(other):
-        for which in range(2):
-            relayed = 2 * other + (1 - core)
-            pltpu.make_async_copy(
-                kv.at[which, relayed], kv.at[which, relayed], kv_recv.at[which, relayed]
-            ).wait()
-        for block in (2 * other, 2 * other + 1):
-            attend(block)
-
-    for other in range(heads):
-        direct = 2 * other + core
-        for which in range(2):
-            landed = kv.at[which, direct]
-            pltpu.make_async_copy(landed, landed, kv_recv.at[which, direct]).wait()
-
-            @pl.when(other != chip)
-            def _():
-                remote(
-                    landed,
-                    landed,
-                    fwd_send.at[which, other],
-                    kv_recv.at[which, direct],
-                    {"seq": sibling},
-                ).start()
-
-        if other > 0:
-            attend_chip(other - 1)
+            pltpu.make_async_copy(result.at[place], mix.at[mine], r_recv.at[mine]).start()
+
     for step in range(1, n_dp):
         source = (dp + step) % n_dp
         came = table_buf.at[source, pl.ds(core * part_nodes, part_nodes)]
-        pltpu.make_async_copy(came, came, table_recv.at[source]).wait()
+        landed(came, table_recv.at[source])
         copy = remote(came, came, table_fwd.at[step], table_relay.at[source], {"seq": sibling})
         copy.start()
         waits.append(copy)
-    attend_chip(heads - 1)
+
+    @pl.when(side == 0)
+    def _():
+        copies = []
+        for step in range(heads):
+            block = heads + (mine + heads - step) % heads
+            landed(query.at[block], q_recv.at[block])
+            offset = pl.multiple_of((n_seq - 1 - block) * tok, tok)
+            result[heads + step] = attend(
+                block,
+                0,
+                key_values(0, heads),
+                key_values(1, heads),
+                bias[:, pl.ds(offset, heads * tok)],
+            )
+            copy = remote(
+                result.at[heads + step],
+                mix_low.at[mine],
+                r_send.at[heads + step],
+                r_low_recv.at[mine],
+                {"seq": block},
+            )
+            copy.start()
+            copies.append(copy)
+        for copy in copies:
+            copy.wait_send()
 
     w_out_copy.wait()
-    for source in range(n_seq):
-        landing = mix.at[source // 2, pl.ds((source % 2) * half, half)]
-        pltpu.make_async_copy(landing, landing, r_recv.at[source]).wait()
-    mixed = jnp.concatenate([mix[head] for head in range(heads)], axis=1).astype(jnp.float32)
+    for source in range(heads):
+        landed(mix.at[source], r_recv.at[source])
+
+    @pl.when(side == 1)
+    def _():
+        for source in range(heads):
+            landed(mix_low.at[source], r_low_recv.at[source])
+
+    mixed = jnp.concatenate(
+        [
+            mix[head].astype(jnp.float32) + mix_low[head].astype(jnp.float32)
+            for head in range(heads)
+        ],
+        axis=1,
+    )
     gated = layer_norm(mixed) * out_gain_ref[...] * gate[...].astype(jnp.float32)
     out = jnp.dot(
         gated.astype(jnp.bfloat16), w_out_buf[...], preferred_element_type=jnp.float32
@@ -367,30 +371,24 @@
 
     for copy in waits:
         copy.wait_send()
-    for other in range(heads):
-        direct = 2 * other + core
-
-        @pl.when(other != chip)
-        def _():
-            for which in range(2):
-                remote(
-                    kv.at[which, direct],
-                    kv.at[which, direct],
-                    fwd_send.at[which, other],
-                    kv_recv.at[which, direct],
-                    {"seq": sibling},
-                ).wait_send()
-
-    for block in range(n_seq):
-
-        @pl.when(me != block)
+    @pl.when(side == 1)
+    def _():
+        for step in range(heads):
+            head = (mine + step) % heads
+            remote(
+                sent.at[0, head], query.at[me], cross_send.at[step], q_recv.at[me], {"seq": head}
+            ).wait_send()
+
+    for place in range(heads):
+
+        @pl.when(mine != place)
         def _():
             remote(
-                result.at[block],
-                mix.at[chip, pl.ds(core * half, half)],
-                r_send.at[block],
-                r_recv.at[me],
-                {"seq": block},
+                result.at[place],
+                mix.at[mine],
+                r_send.at[place],
+                r_recv.at[mine],
+                {"seq": base + place},
             ).wait_send()
 
     for step in far_first(n_seq):
@@ -440,9 +438,7 @@
     heads = rab_slope.shape[0]
     head_dim = width // heads
     nodes = node_table.shape[0]
-    half = tok // 2
     assert n_seq == 2 * heads and tok == BLK
-    window = n_seq // 2 + 2
     part_rows = -(-USERS * n_dp * nodes // LANES // 16) * 16
     vmem = pl.BlockSpec(memory_space=pltpu.VMEM)
     smem = pl.BlockSpec(memory_space=pltpu.SMEM)
@@ -464,11 +460,12 @@
             pltpu.VMEM((n_dp, nodes, width), bf16),
             pltpu.VMEM((3, heads, tok, head_dim), bf16),
             pltpu.VMEM((tok, width), bf16),
-            pltpu.VMEM((2, n_seq, tok, head_dim), bf16),
-            pltpu.VMEM((n_seq, half, head_dim), bf16),
-            pltpu.VMEM((n_seq, half, head_dim), bf16),
+            pltpu.VMEM((2, heads, tok, head_dim), bf16),
+            pltpu.VMEM((n_seq, tok, head_dim), bf16),
+            pltpu.VMEM((n_seq, tok, head_dim), bf16),
             pltpu.VMEM((heads, tok, head_dim), bf16),
-            pltpu.VMEM((half, window * tok), jnp.float32),
+            pltpu.VMEM((heads, tok, head_dim), bf16),
+            pltpu.VMEM((tok, n_seq * tok), jnp.float32),
             pltpu.VMEM((part_rows, LANES), bf16),
             pltpu.VMEM((n_seq, part_rows, LANES), bf16),
             pltpu.VMEM((n_dp * nodes, USERS * beam_nodes.shape[1]), bf16),
@@ -481,12 +478,13 @@
             dma((n_dp,)),
             dma((n_dp,)),
             dma((2, heads)),
-            dma((2, n_seq)),
             dma((2, heads)),
+            dma((heads,)),
+            dma((heads,)),
             dma((n_seq,)),
             dma((n_seq,)),
-            dma((n_seq,)),
-            dma((n_seq,)),
+            dma((heads,)),
+            dma((heads,)),
             dma((n_seq,)),
             dma((n_seq,)),
         ],

time: 46.7 us -> 45.2 us (0.968)
  Pallas kernels: 45.9 us -> 44.4 us
    pallas_call x1, Pallas kernels: 44.2 us -> 42.7 us  [body(): pl.pallas_call(functools.partial(layer_kernel, n_dp, n_seq), out_shape=(j...]
where the time goes in v4:
time: 45.2 us; the launch traced here: 45 us
  Pallas kernels  44.4 us (98%)
  between operations  0.64 us (1%)
    pallas_call x1, Pallas kernels, body(): pl.pallas_call(functools.partial(layer_kernel, n_dp, n_seq), out_shape=(j...  42.7 us
    pallas_call x1, Pallas kernels, body(): pl.pallas_call(hand_over, out_shape=(jax.ShapeDtypeStruct(layer_out.shape...  1.67 us

profile of v4, /device:TPU:0, one launch (start us, length us, event | category | flops | bytes accessed | tf_op | source)
XLA Modules:
  0.0 45.0 jit_solution(13734763434384827563)
XLA Ops:
  0.6 42.7 %shard_map.122 = (bf16[1,128,1024]{2,1,0:T(8,128)(2,1)}, f32[3,64]{1,0:T(4,128)}) custom-call(bf16[1,128,1024]{2,1,0:T(8,128)(2,1)} %x_hbm.1, f32[1,1024]{1,0:T(1,128)} %bitcast.2, bf16[1024,4096]{1,0:T(8,128)(2,1)} %w_proj_ref.1, f32[1,1024]{1,0:T(1,128)} %bitcast.3, bf16[1024,1024]{1,0:T(8,128)(2,1)} %w_out_ref.1, f32[8]{0:T(128)} %slope_ref.1, ...), custom_call_target="tpu_custom_call" | custom-call | tf_op jit(solution)/shard_map/pallas_call | solution.py:448
  43.3 1.7 %shard_map.123 = (bf16[1,128,1024]{2,1,0:T(8,128)(2,1)}, f32[3,64]{1,0:T(4,128)}) custom-call(bf16[1,128,1024]{2,1,0:T(8,128)(2,1)} %get-tuple-element.4.layer_in, f32[3,64]{1,0:T(4,128)} %get-tuple-element.5.scores_in), custom_call_target="tpu_custom_call" | custom-call | tf_op jit(solution)/shard_map/pallas_call | solution.py:507

commit v5 on v4

--- a/solution.py
+++ b/solution.py
@@ -92,6 +92,7 @@
     dp = lax.axis_index("dp")
     side, mine = me // heads, me % heads
     base = side * heads
+    window = heads + 2
     core = me % 2
     sibling = me + 1 - 2 * core
 
@@ -136,7 +137,10 @@
         for piece in range(heads // 2):
             columns = pl.ds(piece * 2 * head_dim, 2 * head_dim)
             out = jnp.dot(normed, w_buf[part, :, columns], preferred_element_type=jnp.float32)
-            store(piece, silu_of_half(0.5 * out).astype(jnp.bfloat16))
+            rows = silu_of_half(0.5 * out)
+            if part == 1:
+                rows = rows * (0.5 * head_dim ** (-0.5))
+            store(piece, rows.astype(jnp.bfloat16))
 
     def store_heads(slot):
         def store(piece, rows):
@@ -226,25 +230,30 @@
     def landed(ref, sem):
         pltpu.make_async_copy(ref, ref, sem).wait()
 
-    def attend(block, first_key, key_rows, value_rows, bias_rows):
+    def attend(block, first_key, low, high, bias_at):
         first = jnp.where(block >= starts[1], starts[1], 0)
         length = jnp.where(block >= starts[1], lengths[1], lengths[0])
         first = jnp.where(block >= starts[2], starts[2], first)
         length = jnp.where(block >= starts[2], lengths[2], length)
-        column = lax.broadcasted_iota(jnp.int32, (1, key_rows.shape[0]), 1) + first_key * tok
-        seen = jnp.where(column >= first * tok, 0.0, OFF)
-        scores = lax.dot_general(
-            query[block], key_rows, (((1,), (1,)), ((), ())), preferred_element_type=jnp.float32
-        )
-        halves = scores * (0.5 * head_dim ** (-0.5)) + bias_rows + seen
-        weights = silu_of_half(halves).astype(jnp.bfloat16)
-        out = jnp.dot(weights, value_rows, preferred_element_type=jnp.float32)
+        queries = query[block]
+        total = jnp.zeros((tok, head_dim), jnp.float32)
+        for at in range(low, high, 2):
+            end = min(at + 2, high)
+            wide = (end - at) * tok
+            keys = kv[0, at:end].reshape(wide, head_dim)
+            values = kv[1, at:end].reshape(wide, head_dim)
+            key_block = lax.broadcasted_iota(jnp.int32, (1, wide), 1) // tok + (first_key + at)
+            seen = jnp.where(key_block >= first, 0.0, OFF)
+            scores = lax.dot_general(
+                queries, keys, (((1,), (1,)), ((), ())), preferred_element_type=jnp.float32
+            )
+            begin = bias_at + (at - low) * tok
+            halves = scores + (bias[:, begin : begin + wide] + seen)
+            weights = silu_of_half(halves).astype(jnp.bfloat16)
+            total += jnp.dot(weights, values, preferred_element_type=jnp.float32)
         row = lax.broadcasted_iota(jnp.int32, (tok, head_dim), 0)
         live = (block - first) * tok + row < length
-        return jnp.where(live, out, 0.0).astype(jnp.bfloat16)
-
-    def key_values(which, count):
-        return kv[which, 0:count].reshape(count * tok, head_dim)
+        return jnp.where(live, total, 0.0).astype(jnp.bfloat16)
 
     for place in range(heads):
         block = base + place
@@ -252,13 +261,7 @@
         for which in range(2):
             landed(kv.at[which, place], kv_recv.at[which, place])
         count = place + 1
-        result[place] = attend(
-            block,
-            base,
-            key_values(0, count),
-            key_values(1, count),
-            bias[:, (n_seq - count) * tok :],
-        )
+        result[place] = attend(block, base, 0, count, (n_seq - count) * tok)
 
         @pl.when(mine != place)
         def _():
@@ -282,16 +285,10 @@
     def _():
         copies = []
         for step in range(heads):
-            block = heads + (mine + heads - step) % heads
+            block = heads + step
             landed(query.at[block], q_recv.at[block])
-            offset = pl.multiple_of((n_seq - 1 - block) * tok, tok)
-            result[heads + step] = attend(
-                block,
-                0,
-                key_values(0, heads),
-                key_values(1, heads),
-                bias[:, pl.ds(offset, heads * tok)],
-            )
+            low = max(0, block + 1 - window)
+            result[block] = attend(block, 0, low, heads, (n_seq - 1 - block + low) * tok)
             copy = remote(
                 result.at[heads + step],
                 mix_low.at[mine],

time: 45.2 us -> 45.7 us (1.011)
  Pallas kernels: 44.4 us -> 44.9 us
    pallas_call x1, Pallas kernels: 42.7 us -> 43.2 us  [body(): pl.pallas_call(functools.partial(layer_kernel, n_dp, n_seq), out_shape=(j...]
where the time goes in v5:
time: 45.7 us; the launch traced here: 45.5 us
  Pallas kernels  44.9 us (98%)
  between operations  0.64 us (1%)
    pallas_call x1, Pallas kernels, body(): pl.pallas_call(functools.partial(layer_kernel, n_dp, n_seq), out_shape=(j...  43.2 us
    pallas_call x1, Pallas kernels, body(): pl.pallas_call(hand_over, out_shape=(jax.ShapeDtypeStruct(layer_out.shape...  1.67 us

profile of v5, /device:TPU:0, one launch (start us, length us, event | category | flops | bytes accessed | tf_op | source)
XLA Modules:
  0.0 45.5 jit_solution(4530912779490693851)
XLA Ops:
  0.6 43.2 %shard_map.122 = (bf16[1,128,1024]{2,1,0:T(8,128)(2,1)}, f32[3,64]{1,0:T(4,128)}) custom-call(bf16[1,128,1024]{2,1,0:T(8,128)(2,1)} %x_hbm.1, f32[1,1024]{1,0:T(1,128)} %bitcast.2, bf16[1024,4096]{1,0:T(8,128)(2,1)} %w_proj_ref.1, f32[1,1024]{1,0:T(1,128)} %bitcast.3, bf16[1024,1024]{1,0:T(8,128)(2,1)} %w_out_ref.1, f32[8]{0:T(128)} %slope_ref.1, ...), custom_call_target="tpu_custom_call" | custom-call | tf_op jit(solution)/shard_map/pallas_call | solution.py:445
  43.8 1.7 %shard_map.123 = (bf16[1,128,1024]{2,1,0:T(8,128)(2,1)}, f32[3,64]{1,0:T(4,128)}) custom-call(bf16[1,128,1024]{2,1,0:T(8,128)(2,1)} %get-tuple-element.4.layer_in, f32[3,64]{1,0:T(4,128)} %get-tuple-element.5.scores_in), custom_call_target="tpu_custom_call" | custom-call | tf_op jit(solution)/shard_map/pallas_call | solution.py:504

commit v6 on v5

--- a/solution.py
+++ b/solution.py
@@ -56,8 +56,8 @@
     table_buf,
     sent,
     gate,
-    kv,
-    query,
+    held,
+    upper,
     result,
     mix,
     mix_low,
@@ -73,11 +73,10 @@
     table_recv,
     table_fwd,
     table_relay,
-    kv_send,
-    kv_recv,
-    q_send,
+    h_send,
+    h_recv,
     cross_send,
-    q_recv,
+    u_recv,
     r_send,
     r_recv,
     r_low_recv,
@@ -118,6 +117,7 @@
     for part in order:
         w_copies[part].start()
 
+    pltpu.make_async_copy(table_ref, table_buf.at[dp], table_sem).start()
     barrier = pltpu.get_barrier_semaphore()
     for step in range(1, n_seq):
         pl.semaphore_signal(
@@ -144,48 +144,46 @@
 
     def store_heads(slot):
         def store(piece, rows):
-            sent[slot, 2 * piece] = rows[:, :head_dim]
-            sent[slot, 2 * piece + 1] = rows[:, head_dim:]
+            sent[2 * piece, slot] = rows[:, :head_dim]
+            sent[2 * piece + 1, slot] = rows[:, head_dim:]
 
         return store
 
     waits = []
-    for slot, landing, send_sem, recv_sem in (
-        (0, query.at[me], q_send, q_recv.at[me]),
-        (1, kv.at[0, mine], kv_send.at[0], kv_recv.at[0, mine]),
-        (2, kv.at[1, mine], kv_send.at[1], kv_recv.at[1, mine]),
-    ):
-        project(slot + 1, store_heads(slot))
-        if slot == 0:
-            pl.semaphore_wait(barrier, n_seq - 1 + n_dp - 1)
+    project(1, store_heads(0))
+    pl.semaphore_wait(barrier, n_seq - 1 + n_dp - 1)
+
+    @pl.when(side == 1)
+    def _():
         for step in range(heads):
             head = (mine + step) % heads
-            if slot == 0:
-
-                @pl.when(side == 1)
-                def _():
-                    remote(
-                        sent.at[0, head],
-                        query.at[me],
-                        cross_send.at[step],
-                        q_recv.at[me],
-                        {"seq": head},
-                    ).start()
-
-            if step == 0:
-                pltpu.make_async_copy(sent.at[slot, head], landing, recv_sem).start()
-            else:
-                copy = remote(
-                    sent.at[slot, head], landing, send_sem.at[step], recv_sem, {"seq": base + head}
-                )
-                copy.start()
-                waits.append(copy)
+            remote(
+                sent.at[head, 0], upper.at[mine], cross_send.at[step], u_recv.at[mine], {"seq": head}
+            ).start()
+
+    project(2, store_heads(1))
+    project(3, store_heads(2))
+    for step in range(heads):
+        head = (mine + step) % heads
+        if step == 0:
+            pltpu.make_async_copy(sent.at[head], held.at[mine], h_recv.at[mine]).start()
+        else:
+            copy = remote(
+                sent.at[head],
+                held.at[mine],
+                h_send.at[step],
+                h_recv.at[mine],
+                {"seq": base + head},
+            )
+            copy.start()
+            waits.append(copy)
 
     part_nodes = nodes // 2
+    pltpu.make_async_copy(table_ref, table_buf.at[dp], table_sem).wait()
     for step in range(1, n_dp):
         own_rows = pl.ds(core * part_nodes, part_nodes)
         copy = remote(
-            table_ref.at[own_rows],
+            table_buf.at[dp, own_rows],
             table_buf.at[dp, own_rows],
             table_send.at[step],
             table_recv.at[dp],
@@ -193,7 +191,6 @@
         )
         copy.start()
         waits.append(copy)
-    pltpu.make_async_copy(table_ref, table_buf.at[dp], table_sem).start()
     w_out_copy = pltpu.make_async_copy(w_out_ref, w_out_buf, w_out_sem)
     w_out_copy.start()
 
@@ -230,18 +227,17 @@
     def landed(ref, sem):
         pltpu.make_async_copy(ref, ref, sem).wait()
 
-    def attend(block, first_key, low, high, bias_at):
+    def attend(block, queries, first_key, low, high, bias_at):
         first = jnp.where(block >= starts[1], starts[1], 0)
         length = jnp.where(block >= starts[1], lengths[1], lengths[0])
         first = jnp.where(block >= starts[2], starts[2], first)
         length = jnp.where(block >= starts[2], lengths[2], length)
-        queries = query[block]
         total = jnp.zeros((tok, head_dim), jnp.float32)
         for at in range(low, high, 2):
             end = min(at + 2, high)
             wide = (end - at) * tok
-            keys = kv[0, at:end].reshape(wide, head_dim)
-            values = kv[1, at:end].reshape(wide, head_dim)
+            keys = held[at:end, 1].reshape(wide, head_dim)
+            values = held[at:end, 2].reshape(wide, head_dim)
             key_block = lax.broadcasted_iota(jnp.int32, (1, wide), 1) // tok + (first_key + at)
             seen = jnp.where(key_block >= first, 0.0, OFF)
             scores = lax.dot_general(
@@ -257,11 +253,9 @@
 
     for place in range(heads):
         block = base + place
-        landed(query.at[block], q_recv.at[block])
-        for which in range(2):
-            landed(kv.at[which, place], kv_recv.at[which, place])
+        landed(held.at[place], h_recv.at[place])
         count = place + 1
-        result[place] = attend(block, base, 0, count, (n_seq - count) * tok)
+        result[place] = attend(block, held[place, 0], base, 0, count, (n_seq - count) * tok)
 
         @pl.when(mine != place)
         def _():
@@ -286,9 +280,11 @@
         copies = []
         for step in range(heads):
             block = heads + step
-            landed(query.at[block], q_recv.at[block])
+            landed(upper.at[step], u_recv.at[step])
             low = max(0, block + 1 - window)
-            result[block] = attend(block, 0, low, heads, (n_seq - 1 - block + low) * tok)
+            result[block] = attend(
+                block, upper[step], 0, low, heads, (n_seq - 1 - block + low) * tok
+            )
             copy = remote(
                 result.at[heads + step],
                 mix_low.at[mine],
@@ -331,7 +327,6 @@
         last = jnp.where(which_user == u, starts[u] * BLK + lengths[u] - 1, last)
     picker = jnp.where(slot == last, 1.0, 0.0).astype(jnp.bfloat16)
     states = jnp.dot(picker, layer_rows, preferred_element_type=jnp.float32).astype(jnp.bfloat16)
-    pltpu.make_async_copy(table_ref, table_buf.at[dp], table_sem).wait()
     for step in range(1, n_dp):
         source = (dp + step) % n_dp
         came = table_buf.at[source, pl.ds((1 - core) * part_nodes, part_nodes)]
@@ -373,7 +368,7 @@
         for step in range(heads):
             head = (mine + step) % heads
             remote(
-                sent.at[0, head], query.at[me], cross_send.at[step], q_recv.at[me], {"seq": head}
+                sent.at[head, 0], upper.at[mine], cross_send.at[step], u_recv.at[mine], {"seq": head}
             ).wait_send()
 
     for place in range(heads):
@@ -455,10 +450,10 @@
             pltpu.VMEM((4, width, width), bf16),
             pltpu.VMEM((width, width), bf16),
             pltpu.VMEM((n_dp, nodes, width), bf16),
-            pltpu.VMEM((3, heads, tok, head_dim), bf16),
+            pltpu.VMEM((heads, 3, tok, head_dim), bf16),
             pltpu.VMEM((tok, width), bf16),
-            pltpu.VMEM((2, heads, tok, head_dim), bf16),
-            pltpu.VMEM((n_seq, tok, head_dim), bf16),
+            pltpu.VMEM((heads, 3, tok, head_dim), bf16),
+            pltpu.VMEM((heads, tok, head_dim), bf16),
             pltpu.VMEM((n_seq, tok, head_dim), bf16),
             pltpu.VMEM((heads, tok, head_dim), bf16),
             pltpu.VMEM((heads, tok, head_dim), bf16),
@@ -474,11 +469,10 @@
             dma((n_dp,)),
             dma((n_dp,)),
             dma((n_dp,)),
-            dma((2, heads)),
-            dma((2, heads)),
             dma((heads,)),
             dma((heads,)),
-            dma((n_seq,)),
+            dma((heads,)),
+            dma((heads,)),
             dma((n_seq,)),
             dma((heads,)),
             dma((heads,)),

time: 45.7 us -> 45.8 us (level)
  no operation moved by 1% of the time
where the time goes in v6:
time: 45.8 us; the launch traced here: 45.6 us
  Pallas kernels  45 us (98%)
  between operations  0.64 us (1%)
    pallas_call x1, Pallas kernels, body(): pl.pallas_call(functools.partial(layer_kernel, n_dp, n_seq), out_shape=(j...  43.3 us
    pallas_call x1, Pallas kernels, body(): pl.pallas_call(hand_over, out_shape=(jax.ShapeDtypeStruct(layer_out.shape...  1.67 us

profile of v6, /device:TPU:0, one launch (start us, length us, event | category | flops | bytes accessed | tf_op | source)
XLA Modules:
  0.0 45.6 jit_solution(11412325099354608913)
XLA Ops:
  0.6 43.3 %shard_map.122 = (bf16[1,128,1024]{2,1,0:T(8,128)(2,1)}, f32[3,64]{1,0:T(4,128)}) custom-call(bf16[1,128,1024]{2,1,0:T(8,128)(2,1)} %x_hbm.1, f32[1,1024]{1,0:T(1,128)} %bitcast.2, bf16[1024,4096]{1,0:T(8,128)(2,1)} %w_proj_ref.1, f32[1,1024]{1,0:T(1,128)} %bitcast.3, bf16[1024,1024]{1,0:T(8,128)(2,1)} %w_out_ref.1, f32[8]{0:T(128)} %slope_ref.1, ...), custom_call_target="tpu_custom_call" | custom-call | tf_op jit(solution)/shard_map/pallas_call | solution.py:440
  44.0 1.7 %shard_map.123 = (bf16[1,128,1024]{2,1,0:T(8,128)(2,1)}, f32[3,64]{1,0:T(4,128)}) custom-call(bf16[1,128,1024]{2,1,0:T(8,128)(2,1)} %get-tuple-element.4.layer_in, f32[3,64]{1,0:T(4,128)} %get-tuple-element.5.scores_in), custom_call_target="tpu_custom_call" | custom-call | tf_op jit(solution)/shard_map/pallas_call | solution.py:498

commit v7 on v6

--- a/solution.py
+++ b/solution.py
@@ -55,7 +55,7 @@
     w_out_buf,
     table_buf,
     sent,
-    gate,
+    normed_ref,
     held,
     upper,
     result,
@@ -132,25 +132,30 @@
     x_rows = x_ref[0].astype(jnp.float32)
     normed = (layer_norm(x_rows) * in_gain_ref[...]).astype(jnp.bfloat16)
 
-    def project(part, store):
-        w_copies[part].wait()
-        for piece in range(heads // 2):
-            columns = pl.ds(piece * 2 * head_dim, 2 * head_dim)
-            out = jnp.dot(normed, w_buf[part, :, columns], preferred_element_type=jnp.float32)
-            rows = silu_of_half(0.5 * out)
-            if part == 1:
-                rows = rows * (0.5 * head_dim ** (-0.5))
-            store(piece, rows.astype(jnp.bfloat16))
-
-    def store_heads(slot):
-        def store(piece, rows):
-            sent[2 * piece, slot] = rows[:, :head_dim]
-            sent[2 * piece + 1, slot] = rows[:, head_dim:]
-
-        return store
+    pieces = heads // 2
+    pair = 2 * head_dim
+    normed_ref[...] = normed
+
+    def project(step, carry):
+        slot, piece = step // pieces, step % pieces
+        part = (slot + 1) % 4
+
+        @pl.when(piece == 0)
+        def _():
+            pltpu.make_async_copy(
+                w_proj_ref.at[:, pl.ds(0, width)], w_buf.at[part], w_sem.at[part]
+            ).wait()
+
+        columns = pl.ds(pl.multiple_of(piece * pair, pair), pair)
+        out = jnp.dot(normed_ref[...], w_buf[part, :, columns], preferred_element_type=jnp.float32)
+        scale = jnp.where(part == 1, 0.5 * head_dim ** (-0.5), 1.0)
+        rows = (silu_of_half(0.5 * out) * scale).astype(jnp.bfloat16)
+        sent[2 * piece, slot] = rows[:, :head_dim]
+        sent[2 * piece + 1, slot] = rows[:, head_dim:]
+        return carry
 
     waits = []
-    project(1, store_heads(0))
+    lax.fori_loop(0, pieces, project, 0)
     pl.semaphore_wait(barrier, n_seq - 1 + n_dp - 1)
 
     @pl.when(side == 1)
@@ -161,15 +166,14 @@
                 sent.at[head, 0], upper.at[mine], cross_send.at[step], u_recv.at[mine], {"seq": head}
             ).start()
 
-    project(2, store_heads(1))
-    project(3, store_heads(2))
+    lax.fori_loop(pieces, 3 * pieces, project, 0)
     for step in range(heads):
         head = (mine + step) % heads
         if step == 0:
-            pltpu.make_async_copy(sent.at[head], held.at[mine], h_recv.at[mine]).start()
+            pltpu.make_async_copy(sent.at[head, 0:3], held.at[mine], h_recv.at[mine]).start()
         else:
             copy = remote(
-                sent.at[head],
+                sent.at[head, 0:3],
                 held.at[mine],
                 h_send.at[step],
                 h_recv.at[mine],
@@ -194,17 +198,19 @@
     w_out_copy = pltpu.make_async_copy(w_out_ref, w_out_buf, w_out_sem)
     w_out_copy.start()
 
-    def store_gate(piece, rows):
-        gate[:, pl.ds(piece * 2 * head_dim, 2 * head_dim)] = rows
-
-    project(0, store_gate)
-
-    row = lax.broadcasted_iota(jnp.int32, bias.shape, 0)
-    column = lax.broadcasted_iota(jnp.int32, bias.shape, 1)
-    gap = (n_seq - 1) * tok + row - column
+    lax.fori_loop(3 * pieces, 4 * pieces, project, 0)
+
     slope = slope_ref[mine]
-    logs = jnp.log(1.0 + jnp.maximum(gap, 0).astype(jnp.float32))
-    bias[...] = jnp.where(gap >= 0, (0.5 * slope) * logs, OFF)
+
+    def place_bias(delta, carry):
+        row = lax.broadcasted_iota(jnp.int32, bias.shape[1:], 0)
+        column = lax.broadcasted_iota(jnp.int32, bias.shape[1:], 1)
+        gap = delta * 2 * tok + row - column
+        logs = jnp.log(1.0 + jnp.maximum(gap, 0).astype(jnp.float32))
+        bias[delta] = jnp.where(gap >= 0, (0.5 * slope) * logs, OFF)
+        return carry
+
+    lax.fori_loop(0, bias.shape[0], place_bias, 0)
 
     @pl.when(side == 0)
     def _():
@@ -227,45 +233,61 @@
     def landed(ref, sem):
         pltpu.make_async_copy(ref, ref, sem).wait()
 
-    def attend(block, queries, first_key, low, high, bias_at):
+    def user_of(block):
         first = jnp.where(block >= starts[1], starts[1], 0)
         length = jnp.where(block >= starts[1], lengths[1], lengths[0])
         first = jnp.where(block >= starts[2], starts[2], first)
         length = jnp.where(block >= starts[2], lengths[2], length)
-        total = jnp.zeros((tok, head_dim), jnp.float32)
-        for at in range(low, high, 2):
-            end = min(at + 2, high)
-            wide = (end - at) * tok
-            keys = held[at:end, 1].reshape(wide, head_dim)
-            values = held[at:end, 2].reshape(wide, head_dim)
-            key_block = lax.broadcasted_iota(jnp.int32, (1, wide), 1) // tok + (first_key + at)
-            seen = jnp.where(key_block >= first, 0.0, OFF)
+        return first, length
+
+    def attend(block, queries, first_key, low, high):
+        row = lax.broadcasted_iota(jnp.int32, (2 * tok, 1), 0)
+        (first, length), (next_first, next_length) = user_of(block), user_of(block + 1)
+        first_row = jnp.where(row < tok, first, next_first)
+        end_row = jnp.where(row < tok, first * tok + length, next_first * tok + next_length)
+        column = lax.broadcasted_iota(jnp.int32, (1, 2 * tok), 1)
+
+        def tile(at, total):
+            keys = held[pl.ds(2 * at, 2), 1].reshape(2 * tok, head_dim)
+            values = held[pl.ds(2 * at, 2), 2].reshape(2 * tok, head_dim)
+            key_block = jnp.where(column < tok, 0, 1) + (first_key + 2 * at)
             scores = lax.dot_general(
                 queries, keys, (((1,), (1,)), ((), ())), preferred_element_type=jnp.float32
             )
-            begin = bias_at + (at - low) * tok
-            halves = scores + (bias[:, begin : begin + wide] + seen)
+            halves = scores + bias[(block - first_key) // 2 - at]
+            halves = jnp.where(key_block >= first_row, halves, OFF)
             weights = silu_of_half(halves).astype(jnp.bfloat16)
-            total += jnp.dot(weights, values, preferred_element_type=jnp.float32)
-        row = lax.broadcasted_iota(jnp.int32, (tok, head_dim), 0)
-        live = (block - first) * tok + row < length
-        return jnp.where(live, total, 0.0).astype(jnp.bfloat16)
-
-    for place in range(heads):
-        block = base + place
-        landed(held.at[place], h_recv.at[place])
-        count = place + 1
-        result[place] = attend(block, held[place, 0], base, 0, count, (n_seq - count) * tok)
-
-        @pl.when(mine != place)
-        def _():
-            remote(
-                result.at[place], mix.at[mine], r_send.at[place], r_recv.at[mine], {"seq": block}
-            ).start()
-
-        @pl.when(mine == place)
-        def _():
-            pltpu.make_async_copy(result.at[place], mix.at[mine], r_recv.at[mine]).start()
+            return total + jnp.dot(weights, values, preferred_element_type=jnp.float32)
+
+        total = lax.fori_loop(low, high, tile, jnp.zeros((2 * tok, head_dim), jnp.float32))
+        live = block * tok + row < end_row
+        rows = jnp.where(live, total, 0.0).astype(jnp.bfloat16)
+        result[pl.ds(block - base, 2)] = rows.reshape(2, tok, head_dim)
+
+    def own_half(at, carry):
+        for place in (2 * at, 2 * at + 1):
+            landed(held.at[place], h_recv.at[place])
+        queries = held[pl.ds(2 * at, 2), 0].reshape(2 * tok, head_dim)
+        attend(base + 2 * at, queries, base, 0, at + 1)
+        for place in (2 * at, 2 * at + 1):
+
+            @pl.when(mine != place)
+            def _():
+                remote(
+                    result.at[place],
+                    mix.at[mine],
+                    r_send.at[place],
+                    r_recv.at[mine],
+                    {"seq": base + place},
+                ).start()
+
+            @pl.when(mine == place)
+            def _():
+                pltpu.make_async_copy(result.at[place], mix.at[mine], r_recv.at[mine]).start()
+
+        return carry
+
+    lax.fori_loop(0, heads // 2, own_half, 0)
 
     for step in range(1, n_dp):
         source = (dp + step) % n_dp
@@ -277,25 +299,31 @@
 
     @pl.when(side == 0)
     def _():
-        copies = []
-        for step in range(heads):
-            block = heads + step
-            landed(upper.at[step], u_recv.at[step])
-            low = max(0, block + 1 - window)
-            result[block] = attend(
-                block, upper[step], 0, low, heads, (n_seq - 1 - block + low) * tok
-            )
-            copy = remote(
-                result.at[heads + step],
+        def low_half(at, carry):
+            for step in (2 * at, 2 * at + 1):
+                landed(upper.at[step], u_recv.at[step])
+            queries = upper[pl.ds(2 * at, 2)].reshape(2 * tok, head_dim)
+            low = jnp.maximum(at + heads // 2 - window // 2, 0)
+            attend(heads + 2 * at, queries, 0, low, heads // 2)
+            for block in (heads + 2 * at, heads + 2 * at + 1):
+                remote(
+                    result.at[block],
+                    mix_low.at[mine],
+                    r_send.at[block],
+                    r_low_recv.at[mine],
+                    {"seq": block},
+                ).start()
+            return carry
+
+        lax.fori_loop(0, heads // 2, low_half, 0)
+        for block in range(heads, n_seq):
+            remote(
+                result.at[block],
                 mix_low.at[mine],
-                r_send.at[heads + step],
+                r_send.at[block],
                 r_low_recv.at[mine],
                 {"seq": block},
-            )
-            copy.start()
-            copies.append(copy)
-        for copy in copies:
-            copy.wait_send()
+            ).wait_send()
 
     w_out_copy.wait()
     for source in range(heads):
@@ -313,11 +341,19 @@
         ],
         axis=1,
     )
-    gated = layer_norm(mixed) * out_gain_ref[...] * gate[...].astype(jnp.float32)
-    out = jnp.dot(
-        gated.astype(jnp.bfloat16), w_out_buf[...], preferred_element_type=jnp.float32
-    )
-    layer_rows = (x_ref[0].astype(jnp.float32) + out).astype(jnp.bfloat16)
+    gate = jnp.concatenate([sent[head, 3] for head in range(heads)], axis=1)
+    gated = layer_norm(mixed) * out_gain_ref[...] * gate.astype(jnp.float32)
+    normed_ref[...] = gated.astype(jnp.bfloat16)
+
+    def project_out(piece, carry):
+        columns = pl.ds(pl.multiple_of(piece * pair, pair), pair)
+        out = jnp.dot(normed_ref[...], w_out_buf[:, columns], preferred_element_type=jnp.float32)
+        layer_ref[0, :, columns] = (x_ref[0, :, columns].astype(jnp.float32) + out).astype(
+            jnp.bfloat16
+        )
+        return carry
+
+    lax.fori_loop(0, pieces, project_out, 0)
 
     rows = 16
     which_user = lax.broadcasted_iota(jnp.int32, (rows, tok), 0)
@@ -326,7 +362,7 @@
     for u in range(USERS):
         last = jnp.where(which_user == u, starts[u] * BLK + lengths[u] - 1, last)
     picker = jnp.where(slot == last, 1.0, 0.0).astype(jnp.bfloat16)
-    states = jnp.dot(picker, layer_rows, preferred_element_type=jnp.float32).astype(jnp.bfloat16)
+    states = jnp.dot(picker, layer_ref[0], preferred_element_type=jnp.float32).astype(jnp.bfloat16)
     for step in range(1, n_dp):
         source = (dp + step) % n_dp
         came = table_buf.at[source, pl.ds((1 - core) * part_nodes, part_nodes)]
@@ -358,8 +394,6 @@
         )
         copy.start()
         waits.append(copy)
-
-    layer_ref[0] = layer_rows
 
     for copy in waits:
         copy.wait_send()
@@ -450,14 +484,14 @@
             pltpu.VMEM((4, width, width), bf16),
             pltpu.VMEM((width, width), bf16),
             pltpu.VMEM((n_dp, nodes, width), bf16),
-            pltpu.VMEM((heads, 3, tok, head_dim), bf16),
+            pltpu.VMEM((heads, 4, tok, head_dim), bf16),
             pltpu.VMEM((tok, width), bf16),
             pltpu.VMEM((heads, 3, tok, head_dim), bf16),
             pltpu.VMEM((heads, tok, head_dim), bf16),
             pltpu.VMEM((n_seq, tok, head_dim), bf16),
             pltpu.VMEM((heads, tok, head_dim), bf16),
             pltpu.VMEM((heads, tok, head_dim), bf16),
-            pltpu.VMEM((tok, n_seq * tok), jnp.float32),
+            pltpu.VMEM((n_seq // 2, 2 * tok, 2 * tok), jnp.float32),
             pltpu.VMEM((part_rows, LANES), bf16),
             pltpu.VMEM((n_seq, part_rows, LANES), bf16),
             pltpu.VMEM((n_dp * nodes, USERS * beam_nodes.shape[1]), bf16),

time: 45.8 us -> 49.2 us (1.074)
  Pallas kernels: 45 us -> 48.4 us
    pallas_call x1, Pallas kernels: 43.3 us -> 46.7 us  [body(): pl.pallas_call(functools.partial(layer_kernel, n_dp, n_seq), out_shape=(j...]
where the time goes in v7:
time: 49.2 us; the launch traced here: 49 us
  Pallas kernels  48.4 us (98%)
  between operations  0.64 us (1%)
    pallas_call x1, Pallas kernels, body(): pl.pallas_call(functools.partial(layer_kernel, n_dp, n_seq), out_shape=(j...  46.7 us
    pallas_call x1, Pallas kernels, body(): pl.pallas_call(hand_over, out_shape=(jax.ShapeDtypeStruct(layer_out.shape...  1.67 us

profile of v7, /device:TPU:0, one launch (start us, length us, event | category | flops | bytes accessed | tf_op | source)
XLA Modules:
  0.0 49.0 jit_solution(4919036248566589895)
XLA Ops:
  0.6 46.7 %shard_map.122 = (bf16[1,128,1024]{2,1,0:T(8,128)(2,1)}, f32[3,64]{1,0:T(4,128)}) custom-call(bf16[1,128,1024]{2,1,0:T(8,128)(2,1)} %x_hbm.1, f32[1,1024]{1,0:T(1,128)} %bitcast.2, bf16[1024,4096]{1,0:T(8,128)(2,1)} %w_proj_ref.1, f32[1,1024]{1,0:T(1,128)} %bitcast.3, bf16[1024,1024]{1,0:T(8,128)(2,1)} %w_out_ref.1, f32[8]{0:T(128)} %slope_ref.1, ...), custom_call_target="tpu_custom_call" | custom-call | tf_op jit(solution)/shard_map/pallas_call | solution.py:474
  47.3 1.7 %shard_map.123 = (bf16[1,128,1024]{2,1,0:T(8,128)(2,1)}, f32[3,64]{1,0:T(4,128)}) custom-call(bf16[1,128,1024]{2,1,0:T(8,128)(2,1)} %get-tuple-element.4.layer_in, f32[3,64]{1,0:T(4,128)} %get-tuple-element.5.scores_in), custom_call_target="tpu_custom_call" | custom-call | tf_op jit(solution)/shard_map/pallas_call | solution.py:532

commit v8 on v5

--- a/solution.py
+++ b/solution.py
@@ -197,11 +197,6 @@
     w_out_copy = pltpu.make_async_copy(w_out_ref, w_out_buf, w_out_sem)
     w_out_copy.start()
 
-    def store_gate(piece, rows):
-        gate[:, pl.ds(piece * 2 * head_dim, 2 * head_dim)] = rows
-
-    project(0, store_gate)
-
     row = lax.broadcasted_iota(jnp.int32, bias.shape, 0)
     column = lax.broadcasted_iota(jnp.int32, bias.shape, 1)
     gap = (n_seq - 1) * tok + row - column
@@ -212,17 +207,6 @@
     @pl.when(side == 0)
     def _():
         mix_low[...] = jnp.zeros_like(mix_low)
-
-    beams = beam_ref[...]
-    subtree = beams >> 6
-    found = jnp.zeros_like(beams)
-    for index in range(map_ref.shape[0]):
-        found = jnp.where(subtree == index, map_ref[index], found)
-    stored = found * SUBT + (beams & (SUBT - 1))
-    per_user = beams.shape[1]
-    stored_row = jnp.concatenate([stored[u : u + 1] for u in range(USERS)], axis=1)
-    node = lax.broadcasted_iota(jnp.int32, onehot.shape, 0)
-    onehot[...] = jnp.where(node == stored_row, 1.0, 0.0).astype(jnp.bfloat16)
 
     starts = [0, blocks_ref[0, 0], blocks_ref[0, 0] + blocks_ref[0, 1]]
     lengths = [(blocks_ref[0, u] - 1) * BLK + tail_ref[0, u] for u in range(USERS)]
@@ -300,6 +284,11 @@
             copies.append(copy)
         for copy in copies:
             copy.wait_send()
+
+    def store_gate(piece, rows):
+        gate[:, pl.ds(piece * 2 * head_dim, 2 * head_dim)] = rows
+
+    project(0, store_gate)
 
     w_out_copy.wait()
     for source in range(heads):
@@ -365,6 +354,17 @@
         waits.append(copy)
 
     layer_ref[0] = layer_rows
+
+    beams = beam_ref[...]
+    subtree = beams >> 6
+    found = jnp.zeros_like(beams)
+    for index in range(map_ref.shape[0]):
+        found = jnp.where(subtree == index, map_ref[index], found)
+    stored = found * SUBT + (beams & (SUBT - 1))
+    per_user = beams.shape[1]
+    stored_row = jnp.concatenate([stored[u : u + 1] for u in range(USERS)], axis=1)
+    node = lax.broadcasted_iota(jnp.int32, onehot.shape, 0)
+    onehot[...] = jnp.where(node == stored_row, 1.0, 0.0).astype(jnp.bfloat16)
 
     for copy in waits:
         copy.wait_send()

time: 45.7 us -> 45.6 us (level)
  no operation moved by 1% of the time
where the time goes in v8:
time: 45.6 us; the launch traced here: 45.5 us
  Pallas kernels  44.8 us (98%)
  between operations  0.64 us (1%)
    pallas_call x1, Pallas kernels, body(): pl.pallas_call(functools.partial(layer_kernel, n_dp, n_seq), out_shape=(j...  43.1 us
    pallas_call x1, Pallas kernels, body(): pl.pallas_call(hand_over, out_shape=(jax.ShapeDtypeStruct(layer_out.shape...  1.67 us

profile of v8, /device:TPU:0, one launch (start us, length us, event | category | flops | bytes accessed | tf_op | source)
XLA Modules:
  0.0 45.5 jit_solution(8850047290142024861)
XLA Ops:
  0.6 43.1 %shard_map.122 = (bf16[1,128,1024]{2,1,0:T(8,128)(2,1)}, f32[3,64]{1,0:T(4,128)}) custom-call(bf16[1,128,1024]{2,1,0:T(8,128)(2,1)} %x_hbm.1, f32[1,1024]{1,0:T(1,128)} %bitcast.2, bf16[1024,4096]{1,0:T(8,128)(2,1)} %w_proj_ref.1, f32[1,1024]{1,0:T(1,128)} %bitcast.3, bf16[1024,1024]{1,0:T(8,128)(2,1)} %w_out_ref.1, f32[8]{0:T(128)} %slope_ref.1, ...), custom_call_target="tpu_custom_call" | custom-call | tf_op jit(solution)/shard_map/pallas_call | solution.py:445
  43.8 1.7 %shard_map.123 = (bf16[1,128,1024]{2,1,0:T(8,128)(2,1)}, f32[3,64]{1,0:T(4,128)}) custom-call(bf16[1,128,1024]{2,1,0:T(8,128)(2,1)} %get-tuple-element.4.layer_in, f32[3,64]{1,0:T(4,128)} %get-tuple-element.5.scores_in), custom_call_target="tpu_custom_call" | custom-call | tf_op jit(solution)/shard_map/pallas_call | solution.py:504
